TPU v7x, 256 devices: a whole 4x4x8 slice. The times are simulated.
256 devices in a mesh: gx: 16 (over y, x), gy: 16 (over z, core).
Axes of the slice: x: 4, y: 4, z: 8, core: 2. Of those that a mesh axis runs over, the one named last changes fastest.
Arguments:
- atom_cell: int32 [16, 16, 4096], P('gx', 'gy'), may hold values from 0 to 49151
- atom_frac: float32 [3, 16, 16, 4096], P(None, 'gx', 'gy'), may hold values from 0 to 1
- atom_charge: float32 [16, 16, 4096], P('gx', 'gy'), may hold values from -6 to 6
- atom_count: int32 [16, 16], P('gx', 'gy'), may hold values from 1024 to 4096, as said below
- fine_kernel: float32 [9, 9, 9], replicated, may hold values from -1.8 to 1.8
- middle_kernel: float32 [9, 9, 9], replicated, may hold values from -0.9 to 0.9
- coarse_kernel: float32 [9, 9, 9], replicated, may hold values from -0.36 to 0.36
Outputs:
- potential: float32 [256, 384, 128], P('gx', 'gy')
- forces: float32 [3, 16, 16, 4096], P(None, 'gx', 'gy')
Inputs may be any that keep to these rules, and one draw needn't show every extreme that they name: `atom_count`: slots at or past a block's count hold no atom. At least one block is full in every draw; about a quarter of the blocks are nearly full and the rest hold a quarter to a half of 4096.
All inputs are finite; a program needn't handle non-finite values.
Results may differ from a plain program's by a relative error of at most 0.0003.
Values sent between devices are 32-bit elements; how exact they have to be, the bound alone decides.
No kernel may reach another device: no remote copies, remote signals or barrier semaphores. Data moves between devices by JAX's collectives and lax.ppermute only.
A program may use at most 128 MiB of HBM per device.

v0:
```python
import jax
import jax.numpy as jnp
from jax import lax
from jax.sharding import PartitionSpec as P

CX = 16
CY = 24
NZ = 128
ATOMS_DEV = 4096
KERNEL = 9


def from_behind(value, axis, steps):
    count = lax.axis_size(axis)
    pairs = [(source, (source + steps) % count) for source in range(count)]
    return lax.ppermute(value, axis, pairs)


def with_halo(block, sides, width):
    for axis, dim in sides:
        count = lax.axis_size(axis)
        forward = [(i, i + 1) for i in range(count - 1)]
        forward.append((count - 1, 0))
        backward = [(target, source) for source, target in forward]
        low = lax.ppermute(
            lax.slice_in_dim(block, block.shape[dim] - width, None, axis=dim), axis, forward
        )
        high = lax.ppermute(lax.slice_in_dim(block, 0, width, axis=dim), axis, backward)
        block = jnp.concatenate([low, block, high], axis=dim)
    return block


def band_tables(kernel, z_size):
    half_width = KERNEL // 2
    tap_index = lax.broadcasted_iota(jnp.int32, (KERNEL, z_size, z_size), 0)
    z_from = lax.broadcasted_iota(jnp.int32, (KERNEL, z_size, z_size), 1)
    z_to = lax.broadcasted_iota(jnp.int32, (KERNEL, z_size, z_size), 2)
    one_hot = (jnp.mod(z_to + tap_index - half_width, z_size) == z_from).astype(jnp.float32)
    tables = jnp.einsum("abc,cij->abij", kernel, one_hot, precision=lax.Precision.HIGHEST)
    return tables.reshape(KERNEL, KERNEL * z_size, z_size)


def convolve(padded, kernel):
    half_width = KERNEL // 2
    block_rows = padded.shape[0] - 2 * half_width
    block_cols = padded.shape[1] - 2 * half_width
    z_size = padded.shape[2]
    tables = band_tables(kernel, z_size)
    running = jnp.zeros((block_rows * block_cols, z_size), jnp.float32)
    for shift_x in range(KERNEL):
        x_slab = padded[shift_x : shift_x + block_rows]
        joined = jnp.concatenate(
            [x_slab[:, shift_y : shift_y + block_cols, :] for shift_y in range(KERNEL)], axis=2
        )
        running = running + jnp.dot(
            joined.reshape(block_rows * block_cols, KERNEL * z_size),
            tables[shift_x],
            preferred_element_type=jnp.float32,
            precision=lax.Precision.HIGHEST,
        )
    return running.reshape(block_rows, block_cols, z_size)


def halve_axis(segment, dimension):
    length = segment.shape[dimension] - 1
    leading = lax.slice_in_dim(segment, 0, length, 2, dimension)
    middle = lax.slice_in_dim(segment, 1, length + 1, 2, dimension)
    trailing = lax.slice_in_dim(segment, 2, length + 1, 2, dimension)
    return 0.5 * leading + middle + 0.5 * trailing


def restrict(padded):
    half_width = KERNEL // 2
    block_rows = padded.shape[0] - 2 * half_width
    block_cols = padded.shape[1] - 2 * half_width
    segment = padded[
        half_width - 1 : half_width + block_rows, half_width - 1 : half_width + block_cols, :
    ]
    segment = halve_axis(halve_axis(segment, 0), 1)
    segment = jnp.concatenate([segment[:, :, -1:], segment], axis=2)
    return halve_axis(segment, 2)


def refine(extended, dimension):
    length = extended.shape[dimension] - 1
    lower_part = lax.slice_in_dim(extended, 0, length, 1, dimension)
    upper_part = lax.slice_in_dim(extended, 1, length + 1, 1, dimension)
    paired = jnp.stack([lower_part, 0.5 * (lower_part + upper_part)], axis=dimension + 1)
    new_shape = list(lower_part.shape)
    new_shape[dimension] = 2 * length
    return paired.reshape(new_shape)


def prolong(extended):
    extended = jnp.concatenate([extended, extended[:, :, :1]], axis=2)
    return refine(refine(refine(extended, 0), 1), 2)


def upper_rim(grid_in):
    wider = jnp.concatenate([grid_in, from_behind(grid_in[:1], "gx", -1)], axis=0)
    return jnp.concatenate([wider, from_behind(wider[:, :1], "gy", -1)], axis=1)


def corner_terms(atom_cell, atom_frac):
    atom_flat = atom_cell.reshape(-1)
    fractions = atom_frac.reshape(3, -1)
    base_x = atom_flat // (CY * NZ)
    base_y = atom_flat // NZ % CY
    base_z = atom_flat % NZ
    corner_ids = []
    weights = []
    slopes = []
    for corner in range(8):
        raised = [corner >> 2 & 1, corner >> 1 & 1, corner & 1]
        factors = [
            fractions[dimension] if raised[dimension] else 1.0 - fractions[dimension]
            for dimension in range(3)
        ]
        sign_list = [1.0 if raised[dimension] else -1.0 for dimension in range(3)]
        flat_index = ((base_x + raised[0]) * (CY + 1) + base_y + raised[1]) * NZ + (
            base_z + raised[2]
        ) % NZ
        corner_ids.append(flat_index)
        weights.append(factors[0] * factors[1] * factors[2])
        slopes.append(
            jnp.stack(
                [
                    sign_list[0] * factors[1] * factors[2],
                    factors[0] * sign_list[1] * factors[2],
                    factors[0] * factors[1] * sign_list[2],
                ]
            )
        )
    return (corner_ids, jnp.stack(weights), slopes)


def per_device(
    atom_cell, atom_frac, atom_charge, atom_count, fine_kernel, middle_kernel, coarse_kernel
):
    corner_ids, weights, slopes = corner_terms(atom_cell, atom_frac)
    slot_index = lax.broadcasted_iota(jnp.int32, (ATOMS_DEV,), 0)
    is_live = slot_index < atom_count.reshape(())
    live_charge = jnp.where(is_live, atom_charge.reshape(-1), 0.0)
    spread_values = weights * live_charge[None]
    spread = jax.ops.segment_sum(
        spread_values.reshape(-1),
        jnp.stack(corner_ids).reshape(-1),
        num_segments=(CX + 1) * (CY + 1) * NZ,
    ).reshape(CX + 1, CY + 1, NZ)
    from_lower_x = from_behind(spread[CX:], "gx", 1)
    folded = jnp.concatenate([spread[:1] + from_lower_x, spread[1:CX]], axis=0)
    from_lower_y = from_behind(folded[:, CY:], "gy", 1)
    fine_charge = jnp.concatenate([folded[:, :1] + from_lower_y, folded[:, 1:CY]], axis=1)
    fine_padded = with_halo(fine_charge, (("gx", 0), ("gy", 1)), 4)
    middle_charge = restrict(fine_padded)
    middle_padded = with_halo(middle_charge, (("gx", 0), ("gy", 1)), 4)
    coarse_charge = restrict(middle_padded)
    coarse_padded = with_halo(coarse_charge, (("gx", 0), ("gy", 1)), 4)
    coarse_potential = convolve(coarse_padded, coarse_kernel)
    wider = jnp.concatenate([coarse_potential, from_behind(coarse_potential[:1], "gx", -1)], axis=0)
    coarse_extended = jnp.concatenate([wider, from_behind(wider[:, :1], "gy", -1)], axis=1)
    middle_potential = convolve(middle_padded, middle_kernel) + prolong(coarse_extended)
    potential = convolve(fine_padded, fine_kernel) + prolong(upper_rim(middle_potential))
    flat_potential = upper_rim(potential).reshape(-1)
    running = jnp.zeros((3, ATOMS_DEV), jnp.float32)
    for corner in range(8):
        running = running + slopes[corner] * flat_potential[corner_ids[corner]][None]
    forces = (-live_charge[None] * running).reshape(3, 1, 1, ATOMS_DEV)
    return (potential, forces)


def solution(mesh):
    return jax.shard_map(
        per_device,
        mesh=mesh,
        in_specs=(
            P("gx", "gy", None),
            P(None, "gx", "gy", None),
            P("gx", "gy", None),
            P("gx", "gy"),
            P(),
            P(),
            P(),
        ),
        out_specs=(P("gx", "gy", None), P(None, "gx", "gy", None)),
        check_vma=False,
    )
```

profile of v0, /device:TPU:127, one launch (start us, length us, event | category | flops | bytes accessed | tf_op | source)
XLA Modules:
  0.0 556.2 jit_solution(1515308399937866674)
XLA Ops:
  6.0 171.0 %scatter_custom_fusion = f32[54400]{0:T(1024)S(1)} fusion(s32[32768]{0:T(1024)S(1)} %bitcast.327, f32[32768]{0:T(1024)S(1)} %bitcast.328, f32[]{:T(128)} %constant.127.clone.1), kind=kCustom, calls=%fused_computation.194 | custom fusion | flops 32768 | bytes 217604 | tf_op jit(solution)/shard_map/scatter-add | solution.py:145
  180.5 3.8 convolution_bitcast_fusion
  184.3 2.9 fusion.115
  200.2 3.5 collective-permute-start.1
  207.3 3.4 collective-permute-start.2
  232.4 3.9 collective-permute-start.4
  249.8 5.2 collective-permute-start.6
  273.5 3.5 collective-permute-start.8
  283.6 4.8 collective-permute-start.10
  313.3 3.5 collective-permute-start.12
  334.9 5.8 %collective-permute-done.14 = f32[1,6,32]{2,1,0:T(8,128)S(1)} collective-permute-done((f32[1,6,32]{2,1,0:T(8,128)S(1)}, f32[1,6,32]{2,1,0:T(8,128)S(1)}, u32[]{:S(2)}, u32[]{:S(2)}) %collective-permute-start.14) | collective-permute-done | bytes 800 | tf_op jit(solution)/shard_map/ppermute | solution.py:16
  341.5 4.6 collective-permute-done.15
  346.9 3.1 convolution_add_fusion.1
  352.7 3.1 convolution_add_fusion
  359.5 5.6 %collective-permute-done.18 = f32[1,24,128]{1,0,2:T(1,128)S(1)} collective-permute-done((f32[1,24,128]{1,0,2:T(1,128)S(1)}, f32[1,24,128]{1,0,2:T(1,128)S(1)}, u32[]{:S(2)}, u32[]{:S(2)}) %collective-permute-start.18) | collective-permute-done | bytes 12320 | tf_op jit(solution)/shard_map/ppermute | solution.py:16
  365.2 4.8 collective-permute-done.19
  370.1 23.0 %gather_fusion.7 = f32[4096]{0:T(1024)S(1)} fusion(f32[54400]{0:T(1024)S(1)} %reshape.1955, s32[4096]{0:T(1024)S(1)} %copy-done.107), kind=kCustom, calls=%fused_computation.7 | custom fusion | bytes 49152 | tf_op jit(solution)/shard_map/gather | solution.py:167
  393.1 23.0 %gather_fusion.6 = f32[4096]{0:T(1024)S(1)} fusion(f32[54400]{0:T(1024)S(1)} %reshape.1955, s32[4096]{0:T(1024)S(1)} %copy-done.108), kind=kCustom, calls=%fused_computation.6 | custom fusion | bytes 49152 | tf_op jit(solution)/shard_map/gather | solution.py:167
  416.2 23.0 %gather_fusion.5 = f32[4096]{0:T(1024)S(1)} fusion(f32[54400]{0:T(1024)S(1)} %reshape.1955, s32[4096]{0:T(1024)S(1)} %copy-done.109), kind=kCustom, calls=%fused_computation.5 | custom fusion | bytes 49152 | tf_op jit(solution)/shard_map/gather | solution.py:167
  439.2 23.0 %gather_fusion.4 = f32[4096]{0:T(1024)S(1)} fusion(f32[54400]{0:T(1024)S(1)} %reshape.1955, s32[4096]{0:T(1024)S(1)} %copy-done.110), kind=kCustom, calls=%fused_computation.4 | custom fusion | bytes 49152 | tf_op jit(solution)/shard_map/gather | solution.py:167
  462.3 23.0 %gather_fusion.3 = f32[4096]{0:T(1024)S(1)} fusion(f32[54400]{0:T(1024)S(1)} %reshape.1955, s32[4096]{0:T(1024)S(1)} %copy-done.111), kind=kCustom, calls=%fused_computation.3 | custom fusion | bytes 49152 | tf_op jit(solution)/shard_map/gather | solution.py:167
  485.4 23.0 %gather_fusion.2 = f32[4096]{0:T(1024)S(1)} fusion(f32[54400]{0:T(1024)S(1)} %reshape.1955, s32[4096]{0:T(1024)S(1)} %copy-done.112), kind=kCustom, calls=%fused_computation.2 | custom fusion | bytes 49152 | tf_op jit(solution)/shard_map/gather | solution.py:167
  508.4 23.0 %gather_fusion.1 = f32[4096]{0:T(1024)S(1)} fusion(f32[54400]{0:T(1024)S(1)} %reshape.1955, s32[4096]{0:T(1024)S(1)} %broadcast_clamp_fusion.6), kind=kCustom, calls=%fused_computation.1 | custom fusion | bytes 49152 | tf_op jit(solution)/shard_map/gather | solution.py:167
  531.7 23.0 %gather_fusion = f32[4096]{0:T(1024)S(1)} fusion(f32[54400]{0:T(1024)S(1)} %reshape.1955, s32[4096]{0:T(1024)S(1)} %broadcast_clamp_fusion.7), kind=kCustom, calls=%fused_computation | custom fusion | bytes 49152 | tf_op jit(solution)/shard_map/gather | solution.py:167
  (474 shorter events, 135.7 us)
Async XLA Ops:
  0.6 179.9 %copy-start = (f32[9,9,9]{2,1,0:T(8,128)S(1)}, f32[9,9,9]{2,1,0:T(8,128)}, u32[]{:S(2)}) copy-start(f32[9,9,9]{2,1,0:T(8,128)} %param.11) | copy-start | bytes 8752
  0.6 176.7 %copy-start.31 = (f32[3,1,1,4096]{3,2,1,0:T(1,128)S(1)}, f32[3,1,1,4096]{3,2,1,0:T(1,128)}, u32[]{:S(2)}) copy-start(f32[3,1,1,4096]{3,2,1,0:T(1,128)} %param.8) | copy-start | bytes 147460
  0.7 178.9 %copy-start.90 = (s32[1,1,4096]{2,1,0:T(1,128)S(1)}, s32[1,1,4096]{2,1,0:T(1,128)}, u32[]{:S(2)}) copy-start(s32[1,1,4096]{2,1,0:T(1,128)} %param.7) | copy-start | bytes 49156
  177.1 21.5 %collective-permute-start = (f32[1,25,128]{2,1,0:T(8,128)S(1)}, f32[1,25,128]{2,1,0:T(8,128)S(1)}, u32[]{:S(2)}, u32[]{:S(2)}) collective-permute-start(f32[1,25,128]{2,1,0:T(8,128)S(1)} %slice_bitcast_fusion.5), channel_id=1, source_target_pairs={{0,16},{16,32},{32,48},{48,64},{64,80},{80,96},{96,112},{112,128},... | collective-permute-start | bytes 38408 | tf_op jit(solution)/shard_map/ppermute | solution.py:16
  200.2 4.5 collective-permute-start.1
  205.6 26.8 %collective-permute-start.3 = (f32[4,24,128]{2,1,0:T(8,128)S(1)}, f32[4,24,128]{2,1,0:T(8,128)S(1)}, u32[]{:S(2)}, u32[]{:S(2)}) collective-permute-start(f32[4,24,128]{2,1,0:T(8,128)S(1)} %get-tuple-element.152), channel_id=1, source_target_pairs={{16,0},{32,16},{48,32},{64,48},{80,64},{96,80},{112,96},{128,112},... | collective-permute-start | bytes 147464 | tf_op jit(solution)/shard_map/ppermute | solution.py:28
  207.3 25.1 %collective-permute-start.2 = (f32[4,24,128]{2,1,0:T(8,128)S(1)}, f32[4,24,128]{2,1,0:T(8,128)S(1)}, u32[]{:S(2)}, u32[]{:S(2)}) collective-permute-start(f32[4,24,128]{2,1,0:T(8,128)S(1)} %get-tuple-element.151), channel_id=1, source_target_pairs={{0,16},{16,32},{32,48},{48,64},{64,80},{80,96},{96,112},{112,128},... | collective-permute-start | bytes 147464 | tf_op jit(solution)/shard_map/ppermute | solution.py:25
  232.4 5.7 %collective-permute-start.5 = (f32[24,4,128]{2,1,0:T(4,128)S(1)}, f32[24,4,128]{2,1,0:T(4,128)S(1)}, u32[]{:S(2)}, u32[]{:S(2)}) collective-permute-start(f32[24,4,128]{2,1,0:T(4,128)S(1)} %get-tuple-element.139), channel_id=1, source_target_pairs={{1,0},{2,1},{3,2},{4,3},{5,4},{6,5},{7,6},{8,7},{9,8},{10,9},{11,1... | collective-permute-start | bytes 147464 | tf_op jit(solution)/shard_map/ppermute | solution.py:28
  232.4 5.6 %collective-permute-start.4 = (f32[24,4,128]{2,1,0:T(4,128)S(1)}, f32[24,4,128]{2,1,0:T(4,128)S(1)}, u32[]{:S(2)}, u32[]{:S(2)}) collective-permute-start(f32[24,4,128]{2,1,0:T(4,128)S(1)} %get-tuple-element.140), channel_id=1, source_target_pairs={{0,1},{1,2},{2,3},{3,4},{4,5},{5,6},{6,7},{7,8},{8,9},{9,10},{10,1... | collective-permute-start | bytes 147464 | tf_op jit(solution)/shard_map/ppermute | solution.py:25
  249.7 23.8 %collective-permute-start.7 = (f32[4,12,64]{2,1,0:T(8,128)S(1)}, f32[4,12,64]{2,1,0:T(8,128)S(1)}, u32[]{:S(2)}, u32[]{:S(2)}) collective-permute-start(f32[4,12,64]{2,1,0:T(8,128)S(1)} %get-tuple-element.320), channel_id=1, source_target_pairs={{16,0},{32,16},{48,32},{64,48},{80,64},{96,80},{112,96},{128,112},... | collective-permute-start | bytes 36872 | tf_op jit(solution)/shard_map/ppermute | solution.py:28
  249.8 23.7 %collective-permute-start.6 = (f32[4,12,64]{2,1,0:T(8,128)S(1)}, f32[4,12,64]{2,1,0:T(8,128)S(1)}, u32[]{:S(2)}, u32[]{:S(2)}) collective-permute-start(f32[4,12,64]{2,1,0:T(8,128)S(1)} %get-tuple-element.319), channel_id=1, source_target_pairs={{0,16},{16,32},{32,48},{48,64},{64,80},{80,96},{96,112},{112,128},... | collective-permute-start | bytes 36872 | tf_op jit(solution)/shard_map/ppermute | solution.py:25
  273.5 5.1 collective-permute-start.9
  273.5 5.1 collective-permute-start.8
  283.5 29.7 %collective-permute-start.11 = (f32[4,6,32]{2,1,0:T(8,128)S(1)}, f32[4,6,32]{2,1,0:T(8,128)S(1)}, u32[]{:S(2)}, u32[]{:S(2)}) collective-permute-start(f32[4,6,32]{2,1,0:T(8,128)S(1)} %multiply_add_fusion.6), channel_id=1, source_target_pairs={{16,0},{32,16},{48,32},{64,48},{80,64},{96,80},{112,96},{128,112},... | collective-permute-start | bytes 9224 | tf_op jit(solution)/shard_map/ppermute | solution.py:28
  283.6 29.6 %collective-permute-start.10 = (f32[4,6,32]{2,1,0:T(8,128)S(1)}, f32[4,6,32]{2,1,0:T(8,128)S(1)}, u32[]{:S(2)}, u32[]{:S(2)}) collective-permute-start(f32[4,6,32]{2,1,0:T(8,128)S(1)} %multiply_add_fusion.6), channel_id=1, source_target_pairs={{0,16},{16,32},{32,48},{48,64},{64,80},{80,96},{96,112},{112,128},... | collective-permute-start | bytes 9224 | tf_op jit(solution)/shard_map/ppermute | solution.py:25
  313.2 5.1 collective-permute-start.13
  313.3 5.0 collective-permute-start.12
  334.6 6.1 %collective-permute-start.14 = (f32[1,6,32]{2,1,0:T(8,128)S(1)}, f32[1,6,32]{2,1,0:T(8,128)S(1)}, u32[]{:S(2)}, u32[]{:S(2)}) collective-permute-start(f32[1,6,32]{2,1,0:T(8,128)S(1)} %slice_bitcast_fusion.8), channel_id=1, source_target_pairs={{0,240},{16,0},{32,16},{48,32},{64,48},{80,64},{96,80},{112,96},{1... | collective-permute-start | bytes 2312 | tf_op jit(solution)/shard_map/ppermute | solution.py:16
  340.7 5.4 collective-permute-start.15
  346.8 5.9 %collective-permute-start.16 = (f32[1,12,64]{2,1,0:T(8,128)S(1)}, f32[1,12,64]{2,1,0:T(8,128)S(1)}, u32[]{:S(2)}, u32[]{:S(2)}) collective-permute-start(f32[1,12,64]{2,1,0:T(8,128)S(1)} %slice.2247), channel_id=1, source_target_pairs={{0,240},{16,0},{32,16},{48,32},{64,48},{80,64},{96,80},{112,96},{1... | collective-permute-start | bytes 9224 | tf_op jit(solution)/shard_map/ppermute | solution.py:16
  352.7 4.2 collective-permute-start.17
  358.6 6.5 %collective-permute-start.18 = (f32[1,24,128]{1,0,2:T(1,128)S(1)}, f32[1,24,128]{1,0,2:T(1,128)S(1)}, u32[]{:S(2)}, u32[]{:S(2)}) collective-permute-start(f32[1,24,128]{1,0,2:T(1,128)S(1)} %slice.2254), channel_id=1, source_target_pairs={{0,240},{16,0},{32,16},{48,32},{64,48},{80,64},{96,80},{112,96},{1... | collective-permute-start | bytes 36872 | tf_op jit(solution)/shard_map/ppermute | solution.py:16
  359.5 33.6 %copy-start.30 = (f32[16,24,128]{2,1,0:T(8,128)}, f32[16,24,128]{2,1,0:T(8,128)S(1)}, u32[]{:S(2)}) copy-start(f32[16,24,128]{2,1,0:T(8,128)S(1)} %copy.134) | copy-start | bytes 589828
  365.2 4.8 collective-permute-start.19
  (109 other events, 1171.1 us)
where the time goes:
time: 561 us; the launch traced here: 556 us
  local copies, waits for them, and re-layouts  262 us (47%)
  other arithmetic  192 us (34%)
  matrix products  40.5 us (7%)
  starting transfers between devices  30.4 us (5%)
  waiting for transfers between devices  27.6 us (5%)
    gather x8, local copies, waits for them, and re-layouts, per_device(): flat_potential[corner_ids[corner]][None]  184 us
    scatter-add x1, other arithmetic, per_device(): jax.ops.segment_sum(spread_values.reshape(-1), jnp.stack(corner_ids).resh...  171 us
    dot_general x27, matrix products, convolve(): jnp.dot(joined.reshape(block_rows * block_cols, KERNEL * z_size), tables[...  33.6 us
    slice x30, local copies, waits for them, and re-layouts, convolve(): tables[shift_x]  26.9 us
    ppermute x6, starting transfers between devices, with_halo(): lax.ppermute(lax.slice_in_dim(block, block.shape[dim] - width, None, axis...  24.3 us
    ppermute x8, waiting for transfers between devices, from_behind(): return lax.ppermute(value, axis, pairs)  24.1 us
    concatenate x19, local copies, waits for them, and re-layouts, convolve(): jnp.concatenate([x_slab[:, shift_y:shift_y + block_cols, :] for shift_y i...  15.6 us
    unnamed x239, local copies, waits for them, and re-layouts  13.4 us
  transfers between devices with their start and end apart: 20, of which 9 were waited for; matrix products, arithmetic and copies ran while one was open for 17% of the time, Pallas kernels for 0%

commit v1 on v0

v1 whole, which is shorter than its diff:
```python
import functools

import jax
import jax.numpy as jnp
import numpy as np
from jax import lax
from jax.experimental import pallas as pl
from jax.experimental.pallas import tpu as pltpu
from jax.sharding import PartitionSpec as P

CX = 16
CY = 24
NZ = 128
ATOMS = 4096
KERNEL = 9
TILE = 512
HIGHEST = lax.Precision.HIGHEST
F32 = jnp.float32
BF16 = jnp.bfloat16
VMEM_LIMIT = 48 * 1024 * 1024


def lanes_of(n, first):
    half = n // 2
    real = [(first + k, k) for k in range(half)]
    imag = [(first + 64 + k, k) for k in range(1, half)]
    return real, imag, first + 64


def forward_table(n, first):
    z = np.arange(n)
    out = np.zeros((n, 128))
    real, imag, top = lanes_of(n, first)
    for lane, k in real:
        out[:, lane] = np.cos(2 * np.pi * k * z / n)
    for lane, k in imag:
        out[:, lane] = -np.sin(2 * np.pi * k * z / n)
    out[:, top] = np.cos(np.pi * z)
    return out


def inverse_table(n, first):
    z = np.arange(n)
    out = np.zeros((128, n))
    real, imag, top = lanes_of(n, first)
    for lane, k in real:
        out[lane] = (1 if k == 0 else 2) / n * np.cos(2 * np.pi * k * z / n)
    for lane, k in imag:
        out[lane] = -2 / n * np.sin(2 * np.pi * k * z / n)
    out[top] = np.cos(np.pi * z) / n
    return out


def tap_tables(n, first):
    c = np.arange(KERNEL) - KERNEL // 2
    direct = np.zeros((KERNEL, 128))
    crossed = np.zeros((KERNEL, 128))
    real, imag, top = lanes_of(n, first)
    for lane, k in real:
        direct[:, lane] = np.cos(2 * np.pi * k * c / n)
        crossed[:, lane] = -np.sin(2 * np.pi * k * c / n)
    for lane, k in imag:
        direct[:, lane] = np.cos(2 * np.pi * k * c / n)
        crossed[:, lane] = np.sin(2 * np.pi * k * c / n)
    direct[:, top] = np.cos(np.pi * c)
    return np.concatenate([direct, crossed], axis=1)


def restrict_z(n):
    out = np.zeros((n, n // 2))
    for i in range(n // 2):
        out[(2 * i - 1) % n, i] += 0.5
        out[2 * i, i] += 1.0
        out[(2 * i + 1) % n, i] += 0.5
    return out


def prolong_z(n):
    return restrict_z(2 * n).T


def tents(fine, step, coarse):
    far = np.abs(np.arange(fine)[None, :] - step * np.arange(coarse)[:, None])
    return np.maximum(0.0, 1.0 - far / step)


def plane_table(step):
    cx, cy = CX // step + 1, CY // step + 1
    along_x = tents(CX + 1, step, cx)
    along_y = tents(CY + 1, step, cy)
    out = np.zeros((9, 16, CX + 1, 32))
    out[:cx, :cy, :, : CY + 1] = along_x[:, None, :, None] * along_y[None, :, None, :]
    return out.reshape(144, (CX + 1) * 32)


def tables():
    planes = np.concatenate([plane_table(2), plane_table(4)], axis=0)
    forward = np.stack(
        [
            forward_table(128, 0),
            restrict_z(128) @ forward_table(64, 0),
            restrict_z(128) @ restrict_z(64) @ forward_table(32, 32),
        ]
    )
    inverse = np.stack(
        [
            inverse_table(128, 0),
            inverse_table(64, 0) @ prolong_z(64),
            inverse_table(32, 32) @ prolong_z(32) @ prolong_z(64),
        ]
    )
    taps = np.stack([tap_tables(128, 0), tap_tables(64, 0), tap_tables(32, 32)])
    return [np.asarray(t, np.float32) for t in (planes, planes.T, forward, inverse, taps)]


def dot(a, b):
    return jnp.dot(a, b, precision=HIGHEST, preferred_element_type=F32)


def split(value):
    high = value.astype(BF16)
    return high, (value - high.astype(F32)).astype(BF16)


def coarse_lanes(shape):
    lane = lax.broadcasted_iota(jnp.int32, shape, len(shape) - 1) % 64
    return lane >= 32


def rows_of(cell_ref, frac_ref, charge_ref, count_ref, t):
    span = pl.ds(t * TILE, TILE)
    cell = cell_ref[0, :, span]
    f = [frac_ref[k, 0, :, span] for k in range(3)]
    slot = lax.broadcasted_iota(jnp.int32, (1, TILE), 1) + t * TILE
    charge = jnp.where(slot < count_ref[0, 0], charge_ref[0, :, span], 0.0)
    return cell, f, charge, span


def one_hot(cell):
    row = lax.broadcasted_iota(jnp.int32, (CX * CY, TILE), 0)
    return jnp.where(row == (cell >> 7), 1.0, 0.0).astype(BF16)


def spread_kernel(
    count_ref, par_ref, cell_ref, frac_ref, charge_ref, planes_ref, forward_ref,
    shat_ref, mc_ref, s1_ref, s2_ref, t1_ref, t2_ref, acc_ref, grid_ref,
):
    acc_ref[...] = jnp.zeros_like(acc_ref)

    def step(t, carry):
        cell, f, charge, _ = rows_of(cell_ref, frac_ref, charge_ref, count_ref, t)
        hot = one_hot(cell)
        z = cell & (NZ - 1)
        plane = lax.broadcasted_iota(jnp.int32, (NZ, TILE), 0)
        at_low = plane == z
        at_high = plane == ((z + 1) & (NZ - 1))
        wx = [1.0 - f[0], f[0]]
        wy = [1.0 - f[1], f[1]]
        wz = [1.0 - f[2], f[2]]
        for ab in range(4):
            flat = charge * wx[ab >> 1] * wy[ab & 1]
            value = jnp.where(at_low, flat * wz[0], jnp.where(at_high, flat * wz[1], 0.0))
            high, low = split(value)
            dims = (((1,), (1,)), ((), ()))
            acc_ref[:, ab * NZ : (ab + 1) * NZ] += lax.dot_general(
                hot, high, dims, preferred_element_type=F32
            ) + lax.dot_general(hot, low, dims, preferred_element_type=F32)
        return carry

    lax.fori_loop(0, ATOMS // TILE, step, 0)
    grid_ref[...] = jnp.zeros_like(grid_ref)
    for ab in range(4):
        a, b = ab >> 1, ab & 1
        for x in range(CX):
            grid_ref[x + a, b : b + CY, :] += acc_ref[
                x * CY : (x + 1) * CY, ab * NZ : (ab + 1) * NZ
            ]
    grid = grid_ref[...].reshape((CX + 1) * 32, NZ)
    shat = dot(grid, forward_ref[0])
    shat_ref[...] = shat.reshape(CX + 1, 32, NZ)
    small = dot(planes_ref[...], grid)
    mc = dot(small[:144], forward_ref[1]) + dot(small[144:], forward_ref[2])
    mc_ref[...] = mc.reshape(9, 16, NZ)

    even = par_ref[0] == 0
    even2 = par_ref[1] == 0
    is_coarse = coarse_lanes((5, 16, NZ))

    def put_low(ref):
        ref[:, :32, :] = shat_ref[0:5]
        ref[:, 32:, :] = mc_ref[0:5]

    def put_high(ref):
        ref[:, :32, :] = shat_ref[12:17]
        ref[:, 32:, :] = jnp.where(is_coarse, mc_ref[0:5], mc_ref[4:9])

    @pl.when(even)
    def _():
        put_high(s1_ref)
        put_low(s2_ref)

    @pl.when(jnp.logical_not(even))
    def _():
        put_low(s1_ref)
        put_high(s2_ref)

    @pl.when(even2)
    def _():
        t1_ref[...] = mc_ref[4]
        t2_ref[...] = mc_ref[0]

    @pl.when(jnp.logical_not(even2))
    def _():
        t1_ref[...] = mc_ref[0]
        t2_ref[...] = mc_ref[4]


def taps_kernel(fine_ref, middle_ref, coarse_ref, taps_ref, pq_ref, pqm_ref):
    for a in range(KERNEL):
        pq_ref[a] = dot(fine_ref[a], taps_ref[0])
        pqm_ref[a] = dot(middle_ref[a], taps_ref[1]) + dot(coarse_ref[a], taps_ref[2])


def merge_kernel(
    par_ref, shat_ref, mc_ref, r1_ref, r2_ref, rt1_ref, rt2_ref,
    e_ref, g_ref, s1_ref, s2_ref,
):
    e_ref[0:4] = jnp.zeros((4, 32, NZ), F32)
    e_ref[21:25] = jnp.zeros((4, 32, NZ), F32)
    e_ref[4:21] = shat_ref[...]
    g_ref[0:4] = jnp.zeros((4, 16, NZ), F32)
    g_ref[13:17] = jnp.zeros((4, 16, NZ), F32)
    g_ref[4:13] = mc_ref[...]
    is_coarse = coarse_lanes((5, 16, NZ))

    def merge(low_ref, high_ref):
        e_ref[0:5] += low_ref[:, :32, :]
        e_ref[20:25] += high_ref[:, :32, :]
        g_ref[0:5] += low_ref[:, 32:, :]
        high = high_ref[:, 32:, :]
        g_ref[12:17] += jnp.where(is_coarse, 0.0, high)
        g_ref[8:13] += jnp.where(is_coarse, high, 0.0)

    def merge2(low_ref, high_ref):
        g_ref[0] += jnp.where(is_coarse[0], low_ref[...], 0.0)
        g_ref[12] += jnp.where(is_coarse[0], high_ref[...], 0.0)

    even = par_ref[0] == 0
    even2 = par_ref[1] == 0

    @pl.when(even)
    def _():
        merge(r2_ref, r1_ref)

    @pl.when(jnp.logical_not(even))
    def _():
        merge(r1_ref, r2_ref)

    @pl.when(even2)
    def _():
        merge2(rt2_ref, rt1_ref)

    @pl.when(jnp.logical_not(even2))
    def _():
        merge2(rt1_ref, rt2_ref)

    def put_low(ref):
        ref[0:25] = e_ref[:, 0:8, :]
        ref[25:42] = g_ref[:, 0:8, :]

    def put_high(ref):
        ref[0:25, 0:5, :] = e_ref[:, 20:25, :]
        ref[0:25, 5:8, :] = jnp.zeros((25, 3, NZ), F32)
        ref[25:42] = jnp.where(
            coarse_lanes((17, 8, NZ)), g_ref[:, 2:10, :], g_ref[:, 8:16, :]
        )

    y_even = par_ref[2] == 0

    @pl.when(y_even)
    def _():
        put_high(s1_ref)
        put_low(s2_ref)

    @pl.when(jnp.logical_not(y_even))
    def _():
        put_low(s1_ref)
        put_high(s2_ref)


def finish_kernel(
    count_ref, par_ref, e_ref, g_ref, r1_ref, r2_ref, pq_ref, pqm_ref,
    cell_ref, frac_ref, charge_ref, planes_ref, inverse_ref,
    pot_ref, force_ref,
    ee_ref, es_ref, gg_ref, gs_ref, bpq_ref, bpqm_ref, out_ref, outm_ref, full_ref, turned_ref,
):
    for ref, wide, src in ((ee_ref, 32, e_ref), (gg_ref, 16, g_ref)):
        ref[:, 0:4, :] = jnp.zeros((ref.shape[0], 4, NZ), F32)
        ref[:, 4 + wide :, :] = jnp.zeros((ref.shape[0], 4, NZ), F32)
        ref[:, 4 : 4 + wide, :] = src[...]
    is_coarse = coarse_lanes((17, 5, NZ))

    def merge(low_ref, high_ref):
        ee_ref[:, 0:5, :] += low_ref[0:25, 0:5, :]
        ee_ref[:, 28:33, :] += high_ref[0:25, 0:5, :]
        gg_ref[:, 0:5, :] += low_ref[25:42, 0:5, :]
        high = high_ref[25:42, 0:5, :]
        gg_ref[:, 16:21, :] += jnp.where(is_coarse, 0.0, high)
        gg_ref[:, 10:15, :] += jnp.where(is_coarse, high, 0.0)

    y_even = par_ref[2] == 0

    @pl.when(y_even)
    def _():
        merge(r2_ref, r1_ref)

    @pl.when(jnp.logical_not(y_even))
    def _():
        merge(r1_ref, r2_ref)

    es_ref[...] = pltpu.roll(ee_ref[...].reshape(25 * 40, NZ), 64, 1).reshape(25, 40, NZ)
    gs_ref[...] = pltpu.roll(gg_ref[...].reshape(17 * 24, NZ), 64, 1).reshape(17, 24, NZ)
    for a in range(KERNEL):
        for b in range(KERNEL):
            for dst, src in ((bpq_ref, pq_ref), (bpqm_ref, pqm_ref)):
                for half in range(2):
                    dst[a, b, half] = jnp.broadcast_to(
                        src[a, b : b + 1, half * NZ : (half + 1) * NZ], (8, NZ)
                    )

    def correlate(v_ref, vs_ref, taps, dst_ref, rows, tiles):
        def step(t, carry):
            acc = [jnp.zeros((8, NZ), F32) for _ in range(rows)]
            for b in range(KERNEL):
                for xin in range(rows + KERNEL - 1):
                    v = v_ref[xin, pl.ds(t * 8 + b, 8), :]
                    vs = vs_ref[xin, pl.ds(t * 8 + b, 8), :]
                    for a in range(KERNEL):
                        x = xin - a
                        if 0 <= x < rows:
                            acc[x] = acc[x] + v * taps[a, b, 0] + vs * taps[a, b, 1]
            for x in range(rows):
                dst_ref[x, pl.ds(t * 8, 8), :] = acc[x]
            return carry

        lax.fori_loop(0, tiles, step, 0)

    correlate(ee_ref, es_ref, bpq_ref, out_ref, CX + 1, 4)
    correlate(gg_ref, gs_ref, bpqm_ref, outm_ref, 9, 2)

    small = outm_ref[...].reshape(144, NZ)
    levels = jnp.concatenate([dot(small, inverse_ref[1]), dot(small, inverse_ref[2])], axis=0)
    full = dot(out_ref[...].reshape((CX + 1) * 32, NZ), inverse_ref[0]) + dot(
        planes_ref[...], levels
    )
    full_ref[...] = full.reshape(CX + 1, 32, NZ)
    pot_ref[...] = full_ref[0:CX, 0:CY, :]
    for ab in range(4):
        a, b = ab >> 1, ab & 1
        part = full_ref[a : a + CX, b : b + CY, :].reshape(CX * CY, NZ).T
        high, low = split(part)
        turned_ref[0, ab * NZ : (ab + 1) * NZ, :] = high
        turned_ref[1, ab * NZ : (ab + 1) * NZ, :] = low

    def step(t, carry):
        cell, f, charge, span = rows_of(cell_ref, frac_ref, charge_ref, count_ref, t)
        hot = one_hot(cell)
        z = cell & (NZ - 1)
        plane = lax.broadcasted_iota(jnp.int32, (NZ, TILE), 0)
        at_low = plane == z
        at_high = plane == ((z + 1) & (NZ - 1))
        corner = []
        for ab in range(4):
            rows = slice(ab * NZ, (ab + 1) * NZ)
            found = jnp.dot(turned_ref[0, rows, :], hot, preferred_element_type=F32) + jnp.dot(
                turned_ref[1, rows, :], hot, preferred_element_type=F32
            )
            corner.append(
                [
                    jnp.sum(jnp.where(mask, found, 0.0), axis=0, keepdims=True)
                    for mask in (at_low, at_high)
                ]
            )
        wx = [1.0 - f[0], f[0]]
        wy = [1.0 - f[1], f[1]]
        wz = [1.0 - f[2], f[2]]
        sign = [-1.0, 1.0]
        sums = [0.0, 0.0, 0.0]
        for a in range(2):
            for b in range(2):
                for e in range(2):
                    v = corner[2 * a + b][e]
                    sums[0] = sums[0] + sign[a] * wy[b] * wz[e] * v
                    sums[1] = sums[1] + wx[a] * sign[b] * wz[e] * v
                    sums[2] = sums[2] + wx[a] * wy[b] * sign[e] * v
        for k in range(3):
            force_ref[k, 0, :, span] = -charge * sums[k]
        return carry

    lax.fori_loop(0, ATOMS // TILE, step, 0)


def call(kernel, outs, args, in_smem, scratch=()):
    return pl.pallas_call(
        kernel,
        out_shape=[jax.ShapeDtypeStruct(shape, F32) for shape in outs],
        in_specs=[
            pl.BlockSpec(memory_space=pltpu.SMEM if k < in_smem else pltpu.VMEM)
            for k in range(len(args))
        ],
        out_specs=[pl.BlockSpec(memory_space=pltpu.VMEM) for _ in outs],
        scratch_shapes=list(scratch),
        compiler_params=pltpu.CompilerParams(vmem_limit_bytes=VMEM_LIMIT),
    )(*args)


def swap(value, axis, first, gap):
    pairs = []
    for i in range(16):
        partner = ((((i - first) % 16) ^ gap) + first) % 16
        pairs.append((i, partner))
    return lax.ppermute(value, axis, pairs)


def per_device(cell, frac, charge, count, fine, middle, coarse):
    planes, planes_t, forward, inverse, taps = (jnp.asarray(t) for t in tables())
    ix, iy = lax.axis_index("gx"), lax.axis_index("gy")
    par = jnp.stack([ix & 1, (ix >> 1) & 1, iy & 1]).astype(jnp.int32)
    shat, mc, s1, s2, t1, t2 = call(
        spread_kernel,
        [(17, 32, NZ), (9, 16, NZ), (5, 48, NZ), (5, 48, NZ), (16, NZ), (16, NZ)],
        (count, par, cell, frac, charge, planes, forward),
        2,
        [pltpu.VMEM((CX * CY, 4 * NZ), F32), pltpu.VMEM((17, 32, NZ), F32)],
    )
    r1 = swap(s1, "gx", 0, 1)
    r2 = swap(s2, "gx", 1, 1)
    rt1 = swap(t1, "gx", 0, 2)
    rt2 = swap(t2, "gx", 2, 2)
    pq, pqm = call(taps_kernel, [(9, 9, 2 * NZ), (9, 9, 2 * NZ)], (fine, middle, coarse, taps), 0)
    e, g, y1, y2 = call(
        merge_kernel,
        [(25, 32, NZ), (17, 16, NZ), (42, 8, NZ), (42, 8, NZ)],
        (par, shat, mc, r1, r2, rt1, rt2),
        1,
    )
    q1 = swap(y1, "gy", 0, 1)
    q2 = swap(y2, "gy", 1, 1)
    pot, force = call(
        finish_kernel,
        [(CX, CY, NZ), (3, 1, 1, ATOMS)],
        (count, par, e, g, q1, q2, pq, pqm, cell, frac, charge, planes_t, inverse),
        2,
        [
            pltpu.VMEM((25, 40, NZ), F32),
            pltpu.VMEM((25, 40, NZ), F32),
            pltpu.VMEM((17, 24, NZ), F32),
            pltpu.VMEM((17, 24, NZ), F32),
            pltpu.VMEM((9, 9, 2, 8, NZ), F32),
            pltpu.VMEM((9, 9, 2, 8, NZ), F32),
            pltpu.VMEM((17, 32, NZ), F32),
            pltpu.VMEM((9, 16, NZ), F32),
            pltpu.VMEM((17, 32, NZ), F32),
            pltpu.VMEM((2, 4 * NZ, CX * CY), BF16),
        ],
    )
    return pot, force


def solution(mesh):
    return jax.shard_map(
        per_device,
        mesh=mesh,
        in_specs=(
            P("gx", "gy", None),
            P(None, "gx", "gy", None),
            P("gx", "gy", None),
            P("gx", "gy"),
            P(),
            P(),
            P(),
        ),
        out_specs=(P("gx", "gy", None), P(None, "gx", "gy", None)),
        check_vma=False,
    )
```

time: 561 us -> 56.6 us (0.10)
  the two profiles are of different devices: /device:TPU:127 before, /device:TPU:4 now
where the time goes in v1:
time: 56.6 us; the launch traced here: 56.3 us
  Pallas kernels  30.1 us (53%)
  starting transfers between devices  12.7 us (22%)
  waiting for transfers between devices  8.43 us (15%)
  local copies, waits for them, and re-layouts  3.61 us (6%)
  between operations  1.4 us (2%)
    pallas_call x4, Pallas kernels, call(): pl.pallas_call(kernel, out_shape=[jax.ShapeDtypeStruct(shape, F32) for sh...  30.1 us
    ppermute x6, starting transfers between devices, swap(): return lax.ppermute(value, axis, pairs)  12.7 us
    ppermute x6, waiting for transfers between devices, swap(): return lax.ppermute(value, axis, pairs)  8.43 us
    unnamed x26, local copies, waits for them, and re-layouts  3.61 us
  transfers between devices with their start and end apart: 6, of which 3 were waited for; matrix products, arithmetic and copies ran while one was open for 0% of the time, Pallas kernels for 1%

profile of v1, /device:TPU:4, one launch (start us, length us, event | category | flops | bytes accessed | tf_op | source)
XLA Modules:
  0.0 56.3 jit_solution(898390596910717124)
XLA Ops:
  1.3 0.1 pad_add_fusion.par_ref
  1.4 1.1 %copy-done.1 = f32[288,544]{1,0:T(8,128)S(1)} copy-done((f32[288,544]{1,0:T(8,128)S(1)}, f32[288,544]{1,0:T(8,128)}, u32[]{:S(2)}) %copy-start.1) | copy-done | bytes 626712
  2.5 0.9 %copy-done.3 = f32[3,128,128]{2,1,0:T(8,128)S(1)} copy-done((f32[3,128,128]{2,1,0:T(8,128)S(1)}, f32[3,128,128]{2,1,0:T(8,128)}, u32[]{:S(2)}) %copy-start.3) | copy-done | bytes 196632
  3.4 0.8 %copy-done.4 = f32[3,1,1,4096]{3,2,1,0:T(1,128)S(1)} copy-done((f32[3,1,1,4096]{3,2,1,0:T(1,128)S(1)}, f32[3,1,1,4096]{3,2,1,0:T(1,128)}, u32[]{:S(2)}) %copy-start.4) | copy-done | bytes 49176
  4.2 0.7 %copy-done.10 = f32[1,1,4096]{2,1,0:T(1,128)S(1)} copy-done((f32[1,1,4096]{2,1,0:T(1,128)S(1)}, f32[1,1,4096]{2,1,0:T(1,128)}, u32[]{:S(2)}) %copy-start.10) | copy-done | bytes 16408
  4.9 11.2 %shard_map.131 = (f32[17,32,128]{2,1,0:T(8,128)S(1)}, f32[9,16,128]{2,1,0:T(8,128)S(1)}, f32[5,48,128]{2,1,0:T(8,128)S(1)}, f32[5,48,128]{2,1,0:T(8,128)S(1)}, f...) custom-call(s32[1,1]{1,0:T(1,128)S(6)} %copy.14.count_ref, s32[3]{0:T(128)S(1)} %pad_add_fusion.par_ref, ...), custom_call_target="tpu_custom_call" | custom-call | tf_op jit(solution)/shard_map/pallas_call | solution.py:404
  16.1 1.3 %collective-permute-start = (f32[5,48,128]{2,1,0:T(8,128)S(1)}, f32[5,48,128]{2,1,0:T(8,128)S(1)}, u32[]{:S(2)}, u32[]{:S(2)}) collective-permute-start(f32[5,48,128]{2,1,0:T(8,128)S(1)} %get-tuple-element.16), channel_id=1, source_target_pairs={{0,16},{16,0},{32,48},{48,32},{64,80},{80,64},{96,112},{112,96},{1... | collective-permute-start | bytes 368648 | tf_op jit(solution)/shard_map/ppermute | solution.py:422
  17.4 1.6 %collective-permute-start.1 = (f32[5,48,128]{2,1,0:T(8,128)S(1)}, f32[5,48,128]{2,1,0:T(8,128)S(1)}, u32[]{:S(2)}, u32[]{:S(2)}) collective-permute-start(f32[5,48,128]{2,1,0:T(8,128)S(1)} %get-tuple-element.17), channel_id=1, source_target_pairs={{0,240},{16,32},{32,16},{48,64},{64,48},{80,96},{96,80},{112,128},... | collective-permute-start | bytes 368648 | tf_op jit(solution)/shard_map/ppermute | solution.py:422
  19.0 3.7 %collective-permute-start.2 = (f32[16,128]{1,0:T(8,128)S(1)}, f32[16,128]{1,0:T(8,128)S(1)}, u32[]{:S(2)}, u32[]{:S(2)}) collective-permute-start(f32[16,128]{1,0:T(8,128)S(1)} %get-tuple-element.18), channel_id=1, source_target_pairs={{0,32},{16,48},{32,0},{48,16},{64,96},{80,112},{96,64},{112,80},{1... | collective-permute-start | bytes 24584 | tf_op jit(solution)/shard_map/ppermute | solution.py:422
  22.7 1.6 %collective-permute-done.2.rt1_ref = f32[16,128]{1,0:T(8,128)S(1)} collective-permute-done((f32[16,128]{1,0:T(8,128)S(1)}, f32[16,128]{1,0:T(8,128)S(1)}, u32[]{:S(2)}, u32[]{:S(2)}) %collective-permute-start.2) | collective-permute-done | bytes 8224 | tf_op jit(solution)/shard_map/ppermute | solution.py:422
  24.4 4.4 %collective-permute-done.3.rt2_ref = f32[16,128]{1,0:T(8,128)S(1)} collective-permute-done((f32[16,128]{1,0:T(8,128)S(1)}, f32[16,128]{1,0:T(8,128)S(1)}, u32[]{:S(2)}, u32[]{:S(2)}) %collective-permute-start.3) | collective-permute-done | bytes 8224 | tf_op jit(solution)/shard_map/ppermute | solution.py:422
  28.8 0.0 collective-permute-done.1.r2_ref
  28.8 0.0 copy-start.7
  28.8 0.0 copy-start.8
  28.8 0.0 copy-start.12
  28.8 0.7 %shard_map.132 = (f32[25,32,128]{2,1,0:T(8,128)S(1)}, f32[17,16,128]{2,1,0:T(8,128)S(1)}, f32[42,8,128]{2,1,0:T(8,128)S(1)}, f32[42,8,128]{2,1,0:T(8,128)S(1)}) custom-call(s32[3]{0:T(128)S(1)} %pad_add_fusion.par_ref, f32[17,32,128]{2,1,0:T(8,128)S(1)} %get-tuple-element.14.shat_ref, f32[9,16,128]{2,1,0:T(8,128)S(1)} %get-tuple-element.15.mc_ref, ...), custom_call_target="tpu_custom_call" | custom-call | tf_op jit(solution)/shard_map/pallas_call | solution.py:404
  29.5 0.0 copy-start.2
  29.5 0.1 collective-permute-start.4
  29.6 0.0 copy-start.5
  29.6 5.9 %collective-permute-start.5 = (f32[42,8,128]{2,1,0:T(8,128)S(1)}, f32[42,8,128]{2,1,0:T(8,128)S(1)}, u32[]{:S(2)}, u32[]{:S(2)}) collective-permute-start(f32[42,8,128]{2,1,0:T(8,128)S(1)} %get-tuple-element.23), channel_id=1, source_target_pairs={{0,15},{1,2},{2,1},{3,4},{4,3},{5,6},{6,5},{7,8},{8,7},{9,10},{10,... | collective-permute-start | bytes 516104 | tf_op jit(solution)/shard_map/ppermute | solution.py:422
  35.6 0.0 copy-start.11
  35.6 0.7 %shard_map.133 = (f32[9,9,256]{2,1,0:T(8,128)S(1)}, f32[9,9,256]{2,1,0:T(8,128)S(1)}) custom-call(f32[9,9,9]{2,1,0:T(8,128)S(1)} %copy-done.6, f32[9,9,9]{2,1,0:T(8,128)S(1)} %copy-done.7, f32[9,9,9]{2,1,0:T(8,128)S(1)} %copy-done.8, f32[3,9,256]{2,1,0:T(8,128)S(1)} %copy-done.12), custom_call_target="tpu_custom_call" | custom-call | tf_op jit(solution)/shard_map/pallas_call | solution.py:404
  36.3 2.4 %collective-permute-done.5.r2_ref = f32[42,8,128]{2,1,0:T(8,128)S(1)} collective-permute-done((f32[42,8,128]{2,1,0:T(8,128)S(1)}, f32[42,8,128]{2,1,0:T(8,128)S(1)}, u32[]{:S(2)}, u32[]{:S(2)}) %collective-permute-start.5) | collective-permute-done | bytes 172064 | tf_op jit(solution)/shard_map/ppermute | solution.py:422
  38.7 17.6 %shard_map.134 = (f32[16,24,128]{2,1,0:T(8,128)}, f32[3,1,1,4096]{3,2,1,0:T(1,128)}) custom-call(s32[1,1]{1,0:T(1,128)S(6)} %copy.14.count_ref, s32[3]{0:T(128)S(1)} %pad_add_fusion.par_ref, f32[25,32,128]{2,1,0:T(8,128)S(1)} %get-tuple-element.20.e_ref, f32[17,16,128]{2,1,0:T(8,128)S(1)} %get-tuple-element.21.g_ref, ...), custom_call_target="tpu_custom_call" | custom-call | tf_op jit(solution)/shard_map/pallas_call | solution.py:404
  (19 shorter events, 0.0 us)
Async XLA Ops:
  0.6 0.7 %copy-start.9 = (s32[1,1,4096]{2,1,0:T(1,128)S(1)}, s32[1,1,4096]{2,1,0:T(1,128)}, u32[]{:S(2)}) copy-start(s32[1,1,4096]{2,1,0:T(1,128)} %cell_ref.3) | copy-start | bytes 49156
  1.4 1.1 %copy-start.1 = (f32[288,544]{1,0:T(8,128)S(1)}, f32[288,544]{1,0:T(8,128)}, u32[]{:S(2)}) copy-start(f32[288,544]{1,0:T(8,128)} %constant.19.clone.planes_ref) | copy-start | bytes 1880068
  2.5 0.9 %copy-start.3 = (f32[3,128,128]{2,1,0:T(8,128)S(1)}, f32[3,128,128]{2,1,0:T(8,128)}, u32[]{:S(2)}) copy-start(f32[3,128,128]{2,1,0:T(8,128)} %constant.21.clone.forward_ref) | copy-start | bytes 589828
  3.4 0.8 %copy-start.4 = (f32[3,1,1,4096]{3,2,1,0:T(1,128)S(1)}, f32[3,1,1,4096]{3,2,1,0:T(1,128)}, u32[]{:S(2)}) copy-start(f32[3,1,1,4096]{3,2,1,0:T(1,128)} %frac_ref.3) | copy-start | bytes 147460
  4.2 0.7 %copy-start.10 = (f32[1,1,4096]{2,1,0:T(1,128)S(1)}, f32[1,1,4096]{2,1,0:T(1,128)}, u32[]{:S(2)}) copy-start(f32[1,1,4096]{2,1,0:T(1,128)} %charge_ref.3) | copy-start | bytes 49156
  4.9 33.7 %copy-start = (f32[544,288]{1,0:T(8,128)S(1)}, f32[544,288]{1,0:T(8,128)}, u32[]{:S(2)}) copy-start(f32[544,288]{1,0:T(8,128)} %constant.20.clone.planes_ref) | copy-start | bytes 1880068
  16.1 12.7 %collective-permute-start = (f32[5,48,128]{2,1,0:T(8,128)S(1)}, f32[5,48,128]{2,1,0:T(8,128)S(1)}, u32[]{:S(2)}, u32[]{:S(2)}) collective-permute-start(f32[5,48,128]{2,1,0:T(8,128)S(1)} %get-tuple-element.16), channel_id=1, source_target_pairs={{0,16},{16,0},{32,48},{48,32},{64,80},{80,64},{96,112},{112,96},{1... | collective-permute-start | bytes 368648 | tf_op jit(solution)/shard_map/ppermute | solution.py:422
  17.4 11.4 %collective-permute-start.1 = (f32[5,48,128]{2,1,0:T(8,128)S(1)}, f32[5,48,128]{2,1,0:T(8,128)S(1)}, u32[]{:S(2)}, u32[]{:S(2)}) collective-permute-start(f32[5,48,128]{2,1,0:T(8,128)S(1)} %get-tuple-element.17), channel_id=1, source_target_pairs={{0,240},{16,32},{32,16},{48,64},{64,48},{80,96},{96,80},{112,128},... | collective-permute-start | bytes 368648 | tf_op jit(solution)/shard_map/ppermute | solution.py:422
  19.0 5.4 %collective-permute-start.2 = (f32[16,128]{1,0:T(8,128)S(1)}, f32[16,128]{1,0:T(8,128)S(1)}, u32[]{:S(2)}, u32[]{:S(2)}) collective-permute-start(f32[16,128]{1,0:T(8,128)S(1)} %get-tuple-element.18), channel_id=1, source_target_pairs={{0,32},{16,48},{32,0},{48,16},{64,96},{80,112},{96,64},{112,80},{1... | collective-permute-start | bytes 24584 | tf_op jit(solution)/shard_map/ppermute | solution.py:422
  22.7 6.1 %collective-permute-start.3 = (f32[16,128]{1,0:T(8,128)S(1)}, f32[16,128]{1,0:T(8,128)S(1)}, u32[]{:S(2)}, u32[]{:S(2)}) collective-permute-start(f32[16,128]{1,0:T(8,128)S(1)} %get-tuple-element.19), channel_id=1, source_target_pairs={{0,224},{16,240},{32,64},{48,80},{64,32},{80,48},{96,128},{112,144... | collective-permute-start | bytes 24584 | tf_op jit(solution)/shard_map/ppermute | solution.py:422
  28.8 6.8 %copy-start.6 = (f32[9,9,9]{2,1,0:T(8,128)S(1)}, f32[9,9,9]{2,1,0:T(8,128)}, u32[]{:S(2)}) copy-start(f32[9,9,9]{2,1,0:T(8,128)} %fine_ref.1) | copy-start | bytes 8752
  28.8 6.8 %copy-start.7 = (f32[9,9,9]{2,1,0:T(8,128)S(1)}, f32[9,9,9]{2,1,0:T(8,128)}, u32[]{:S(2)}) copy-start(f32[9,9,9]{2,1,0:T(8,128)} %middle_ref.1) | copy-start | bytes 8752
  28.8 6.8 %copy-start.8 = (f32[9,9,9]{2,1,0:T(8,128)S(1)}, f32[9,9,9]{2,1,0:T(8,128)}, u32[]{:S(2)}) copy-start(f32[9,9,9]{2,1,0:T(8,128)} %coarse_ref.1) | copy-start | bytes 8752
  28.8 6.8 %copy-start.12 = (f32[3,9,256]{2,1,0:T(8,128)S(1)}, f32[3,9,256]{2,1,0:T(8,128)}, u32[]{:S(2)}) copy-start(f32[3,9,256]{2,1,0:T(8,128)} %constant.23.clone.taps_ref) | copy-start | bytes 82948
  29.5 9.2 %copy-start.2 = (f32[3,128,128]{2,1,0:T(8,128)S(1)}, f32[3,128,128]{2,1,0:T(8,128)}, u32[]{:S(2)}) copy-start(f32[3,128,128]{2,1,0:T(8,128)} %constant.22.clone.inverse_ref) | copy-start | bytes 589828
  29.5 6.8 %collective-permute-start.4 = (f32[42,8,128]{2,1,0:T(8,128)S(1)}, f32[42,8,128]{2,1,0:T(8,128)S(1)}, u32[]{:S(2)}, u32[]{:S(2)}) collective-permute-start(f32[42,8,128]{2,1,0:T(8,128)S(1)} %get-tuple-element.22), channel_id=1, source_target_pairs={{0,1},{1,0},{2,3},{3,2},{4,5},{5,4},{6,7},{7,6},{8,9},{9,8},{10,11... | collective-permute-start | bytes 516104 | tf_op jit(solution)/shard_map/ppermute | solution.py:422
  29.6 9.1 %copy-start.5 = (f32[3,1,1,4096]{3,2,1,0:T(1,128)S(1)}, f32[3,1,1,4096]{3,2,1,0:T(1,128)}, u32[]{:S(2)}) copy-start(f32[3,1,1,4096]{3,2,1,0:T(1,128)} %frac_ref.3) | copy-start | bytes 147460
  29.6 9.0 %collective-permute-start.5 = (f32[42,8,128]{2,1,0:T(8,128)S(1)}, f32[42,8,128]{2,1,0:T(8,128)S(1)}, u32[]{:S(2)}, u32[]{:S(2)}) collective-permute-start(f32[42,8,128]{2,1,0:T(8,128)S(1)} %get-tuple-element.23), channel_id=1, source_target_pairs={{0,15},{1,2},{2,1},{3,4},{4,3},{5,6},{6,5},{7,8},{8,7},{9,10},{10,... | collective-permute-start | bytes 516104 | tf_op jit(solution)/shard_map/ppermute | solution.py:422
  35.6 3.1 %copy-start.11 = (f32[1,1,4096]{2,1,0:T(1,128)S(1)}, f32[1,1,4096]{2,1,0:T(1,128)}, u32[]{:S(2)}) copy-start(f32[1,1,4096]{2,1,0:T(1,128)} %charge_ref.3) | copy-start | bytes 49156

commit v2 on v1

v2 whole, which is shorter than its diff:
```python
import functools

import jax
import jax.numpy as jnp
import numpy as np
from jax import lax
from jax.experimental import pallas as pl
from jax.experimental.pallas import tpu as pltpu
from jax.sharding import PartitionSpec as P

CX = 16
CY = 24
NZ = 128
ATOMS = 4096
KERNEL = 9
TILE = 1024
HIGHEST = lax.Precision.HIGHEST
F32 = jnp.float32
BF16 = jnp.bfloat16
VMEM_LIMIT = 48 * 1024 * 1024


LINE = CY + KERNEL
FIRST = {128: 0, 64: 65, 32: 98}


def forward_table(n):
    z, k = np.arange(n)[:, None], np.arange(n // 2 + 1)[None, :]
    turn = np.exp(-2j * np.pi * k * z / n)
    return placed(turn, n)


def placed(turn, n):
    out = np.zeros((turn.shape[0], 256))
    first, count = FIRST[n], n // 2 + 1
    out[:, first : first + count] = turn.real
    out[:, 128 + first : 128 + first + count] = turn.imag
    return out


def inverse_table(n):
    z, k = np.arange(n)[:, None], np.arange(n // 2 + 1)[None, :]
    weight = np.where((k == 0) | (k == n // 2), 1.0, 2.0) / n
    return placed(weight * np.exp(-2j * np.pi * k * z / n), n).T


def tap_tables(n):
    c, k = np.arange(KERNEL)[:, None] - KERNEL // 2, np.arange(n // 2 + 1)[None, :]
    return placed(np.exp(2j * np.pi * k * c / n), n)


def line_tables():
    k = np.arange(LINE)
    forward = np.zeros((40, 40), complex)
    forward[:LINE, :LINE] = np.exp(-2j * np.pi * np.outer(k, k) / LINE)
    back = np.zeros((32, 40), complex)
    back[: CY + 1, :LINE] = np.exp(2j * np.pi * np.outer(np.arange(CY + 1), k) / LINE) / LINE
    spread = np.zeros((40, KERNEL), complex)
    spread[:LINE] = np.exp(2j * np.pi * np.outer(k, np.arange(KERNEL)) / LINE)

    def both(table, copies):
        return np.concatenate(
            [np.kron(np.eye(copies), table.real), np.kron(np.eye(copies), table.imag)], axis=0
        )

    return both(forward, 5), both(back, 6), both(spread, 1)


def restrict_z(n):
    out = np.zeros((n, n // 2))
    for i in range(n // 2):
        out[(2 * i - 1) % n, i] += 0.5
        out[2 * i, i] += 1.0
        out[(2 * i + 1) % n, i] += 0.5
    return out


def prolong_z(n):
    return restrict_z(2 * n).T


def tents(fine, step, coarse):
    far = np.abs(np.arange(fine)[None, :] - step * np.arange(coarse)[:, None])
    return np.maximum(0.0, 1.0 - far / step)


def plane_table(step):
    cx, cy = CX // step + 1, CY // step + 1
    along_x = tents(CX + 1, step, cx)
    along_y = tents(CY + 1, step, cy)
    out = np.zeros((9, 16, CX + 1, 32))
    out[:cx, :cy, :, : CY + 1] = along_x[:, None, :, None] * along_y[None, :, None, :]
    return out.reshape(144, (CX + 1) * 32)


def halves(table):
    table = np.asarray(table, np.float32)
    high = table.astype(BF16)
    return np.stack([high, (table - high.astype(np.float32)).astype(BF16)])


def tables():
    small = np.zeros((128, 256))
    small[:64] = forward_table(64)
    small[64:96] = forward_table(32)
    line, back, spread = line_tables()
    inverse = np.concatenate(
        [
            inverse_table(64) @ prolong_z(64),
            inverse_table(32) @ prolong_z(32) @ prolong_z(64),
        ],
        axis=1,
    )
    parts = {
        "plane2": np.asarray(plane_table(2).T, BF16),
        "plane4": np.asarray(plane_table(4).T, BF16),
    }
    for name, table in (
        ("forward", forward_table(128)),
        ("small", small),
        ("line", line),
        ("back", back),
        ("inverse", inverse_table(128)),
        ("levels", inverse),
        ("spread", spread),
        ("tap128", tap_tables(128)),
        ("tap64", tap_tables(64)),
        ("tap32", tap_tables(32)),
    ):
        parts[name + "_high"], parts[name + "_low"] = halves(table)
    places = {}
    blocks = []
    start = 0
    for name, part in parts.items():
        rows, cols = part.shape
        whole = -(-rows // 16) * 16
        places[name] = (start, whole, cols)
        blocks.append(np.pad(part, ((0, whole - rows), (0, 256 - cols))))
        start += whole
    return np.concatenate(blocks, axis=0), places


PACKED, PLACES = tables()


def table(ref, name, first=0):
    if name + "_high" in PLACES:
        return table(ref, name + "_high", first), table(ref, name + "_low", first)
    start, rows, cols = PLACES[name]
    return ref[start - first : start - first + rows, :cols]


def whole(ref, name, first):
    high, low = table(ref, name, first)
    return high.astype(F32) + low.astype(F32)


def dot(a, b):
    return jnp.dot(a, b, precision=HIGHEST, preferred_element_type=F32)


def dot_exact(table, value):
    high, low = split(value)
    return jnp.dot(table, high, preferred_element_type=F32) + jnp.dot(
        table, low, preferred_element_type=F32
    )


def split(value):
    high = value.astype(BF16)
    return high, (value - high.astype(F32)).astype(BF16)


def dot3(a, b):
    total = jnp.dot(a[0], b[0], preferred_element_type=F32)
    total += jnp.dot(a[0], b[1], preferred_element_type=F32)
    return total + jnp.dot(a[1], b[0], preferred_element_type=F32)


def tent(far, step):
    return jnp.maximum(step - jnp.abs(far), 0)


def plane_tents(step):
    row = lax.broadcasted_iota(jnp.int32, (144, (CX + 1) * 32), 0)
    col = lax.broadcasted_iota(jnp.int32, (144, (CX + 1) * 32), 1)
    along_x = tent((col >> 5) - step * (row >> 4), step)
    along_y = tent((col & 31) - step * (row & 15), step)
    return ((along_x * along_y).astype(F32) * (1.0 / step**2)).astype(BF16)


def depth_tents(step, first):
    row = lax.broadcasted_iota(jnp.int32, (NZ, NZ), 0)
    col = lax.broadcasted_iota(jnp.int32, (NZ, NZ), 1) - first
    far = (row - step * col) & (NZ - 1)
    weight = tent(far, step) + tent(NZ - far, step)
    weight = jnp.where((col >= 0) & (col < NZ // step), weight, 0)
    return (weight.astype(F32) * (1.0 / step)).astype(BF16)


def dot_right(value, table):
    high, low = split(value)
    return jnp.dot(high, table, preferred_element_type=F32) + jnp.dot(
        low, table, preferred_element_type=F32
    )


def coarse_lanes(shape):
    return lax.broadcasted_iota(jnp.int32, shape, len(shape) - 1) >= 64


def rows_of(cell_ref, frac_ref, charge_ref, t):
    span = pl.ds(t * TILE, TILE)
    cell = cell_ref[0, :, span]
    f = [frac_ref[k, 0, :, span] for k in range(3)]
    return cell, f, charge_ref[0, :, span], span


def one_hot(cell):
    row = lax.broadcasted_iota(jnp.int32, (CX * CY, TILE), 0)
    return jnp.where(row == (cell >> 7), 1.0, 0.0).astype(BF16)


def spread_kernel(
    par_ref, count_ref, cell_hbm, frac_hbm, charge_hbm,
    grid_ref, mc_ref, s1_ref, s2_ref, t1_ref, t2_ref, live_ref,
    cell_ref, frac_ref, charge_ref, planes_ref, acc_ref, sems,
):
    copies = [
        pltpu.make_async_copy(src, dst, sems.at[k])
        for k, (src, dst) in enumerate(
            (
                (cell_hbm, cell_ref),
                (frac_hbm, frac_ref),
                (charge_hbm, charge_ref),
            )
        )
    ]
    for copy in copies:
        copy.start()
    acc_ref[...] = jnp.zeros_like(acc_ref)
    grid_ref[...] = jnp.zeros_like(grid_ref)
    planes_ref[0:144] = plane_tents(2)
    planes_ref[144:288] = plane_tents(4)
    for copy in copies:
        copy.wait()
    slot = lax.broadcasted_iota(jnp.int32, (1, ATOMS), 1)
    live_ref[0] = jnp.where(slot < count_ref[0, 0], charge_ref[0], 0.0)

    def step(t, carry):
        cell, f, charge, _ = rows_of(cell_ref, frac_ref, live_ref, t)
        hot = one_hot(cell)
        z = cell & (NZ - 1)
        plane = lax.broadcasted_iota(jnp.int32, (NZ, TILE), 0)
        at_low = plane == z
        at_high = plane == ((z + 1) & (NZ - 1))
        wx = [1.0 - f[0], f[0]]
        wy = [1.0 - f[1], f[1]]
        wz = [1.0 - f[2], f[2]]
        highs = []
        lows = []
        for ab in range(4):
            flat = charge * wx[ab >> 1] * wy[ab & 1]
            weights = [flat * wz[e] for e in range(2)]
            tops = [w.astype(BF16).astype(F32) for w in weights]
            for group, (w0, w1) in (
                (highs, tops),
                (lows, [w - t for w, t in zip(weights, tops)]),
            ):
                group.append(
                    jnp.where(at_low, w0, jnp.where(at_high, w1, 0.0)).astype(BF16)
                )
        dims = (((1,), (1,)), ((), ()))
        acc_ref[...] += sum(
            lax.dot_general(
                hot, jnp.concatenate(group, axis=0), dims, preferred_element_type=F32
            )
            for group in (highs, lows)
        )
        return carry

    lax.fori_loop(0, ATOMS // TILE, step, 0)
    for ab in range(4):
        a, b = ab >> 1, ab & 1
        for x in range(CX):
            grid_ref[x + a, b : b + CY, :] += acc_ref[
                x * CY : (x + 1) * CY, ab * NZ : (ab + 1) * NZ
            ]
    grid = grid_ref[...].reshape((CX + 1) * 32, NZ)
    small = dot_exact(planes_ref[...], grid)
    mc = dot_right(small[:144], depth_tents(2, 0)) + dot_right(small[144:], depth_tents(4, 64))
    mc_ref[...] = mc.reshape(9, 16, NZ)

    even = par_ref[0] == 0
    even2 = par_ref[1] == 0
    is_coarse = coarse_lanes((5, 16, NZ))

    def put_low(ref):
        ref[:, :32, :] = grid_ref[0:5]
        ref[:, 32:, :] = mc_ref[0:5]

    def put_high(ref):
        ref[:, :32, :] = grid_ref[12:17]
        ref[:, 32:, :] = jnp.where(is_coarse, mc_ref[0:5], mc_ref[4:9])

    @pl.when(even)
    def _():
        put_high(s1_ref)
        put_low(s2_ref)

    @pl.when(jnp.logical_not(even))
    def _():
        put_low(s1_ref)
        put_high(s2_ref)

    @pl.when(even2)
    def _():
        t1_ref[...] = mc_ref[4]
        t2_ref[...] = mc_ref[0]

    @pl.when(jnp.logical_not(even2))
    def _():
        t1_ref[...] = mc_ref[0]
        t2_ref[...] = mc_ref[4]


def taps_kernel(
    fine_hbm, middle_hbm, coarse_hbm, packed_hbm, live_ref, h_ref,
    fine_ref, middle_ref, coarse_ref, packed_ref, sems,
):
    first = PLACES["spread_high"][0]
    pairs = (
        (fine_hbm, fine_ref),
        (middle_hbm, middle_ref),
        (coarse_hbm, coarse_ref),
        (packed_hbm.at[first : PACKED.shape[0]], packed_ref),
    )
    copies = [pltpu.make_async_copy(*pair, sems.at[k]) for k, pair in enumerate(pairs)]
    for copy in copies:
        copy.start()
    for copy in copies:
        copy.wait()
    levels = [
        (ref, whole(packed_ref, name, first)[:KERNEL])
        for ref, name in ((fine_ref, "tap128"), (middle_ref, "tap64"), (coarse_ref, "tap32"))
    ]
    spread = whole(packed_ref, "spread", first)
    for a in range(KERNEL):
        along_z = sum(dot(ref[a], tap) for ref, tap in levels)
        both = dot(spread, along_z)
        h_ref[a, :, :NZ] = both[:40, :NZ] - both[40:, NZ:]
        h_ref[a, :, NZ:] = both[:40, NZ:] + both[40:, :NZ]


def merge_kernel(
    par_ref, shat_ref, mc_ref, r1_ref, r2_ref, rt1_ref, rt2_ref, h_ref,
    e_ref, g_ref, s1_ref, s2_ref,
):
    e_ref[0:4] = jnp.zeros((4, 32, NZ), F32)
    e_ref[21:25] = jnp.zeros((4, 32, NZ), F32)
    e_ref[4:21] = shat_ref[...]
    g_ref[0:4] = jnp.zeros((4, 16, NZ), F32)
    g_ref[13:17] = jnp.zeros((4, 16, NZ), F32)
    g_ref[4:13] = mc_ref[...]
    is_coarse = coarse_lanes((5, 16, NZ))

    def merge(low_ref, high_ref):
        e_ref[0:5] += low_ref[:, :32, :]
        e_ref[20:25] += high_ref[:, :32, :]
        g_ref[0:5] += low_ref[:, 32:, :]
        high = high_ref[:, 32:, :]
        g_ref[12:17] += jnp.where(is_coarse, 0.0, high)
        g_ref[8:13] += jnp.where(is_coarse, high, 0.0)

    def merge2(low_ref, high_ref):
        g_ref[0] += jnp.where(is_coarse[0], low_ref[...], 0.0)
        g_ref[12] += jnp.where(is_coarse[0], high_ref[...], 0.0)

    even = par_ref[0] == 0
    even2 = par_ref[1] == 0

    @pl.when(even)
    def _():
        merge(r2_ref, r1_ref)

    @pl.when(jnp.logical_not(even))
    def _():
        merge(r1_ref, r2_ref)

    @pl.when(even2)
    def _():
        merge2(rt2_ref, rt1_ref)

    @pl.when(jnp.logical_not(even2))
    def _():
        merge2(rt1_ref, rt2_ref)

    def put_low(ref):
        ref[0:25] = e_ref[:, 0:8, :]
        ref[25:42] = g_ref[:, 0:8, :]

    def put_high(ref):
        ref[0:25, 0:5, :] = e_ref[:, 20:25, :]
        ref[0:25, 5:8, :] = jnp.zeros((25, 3, NZ), F32)
        ref[25:42] = jnp.where(
            coarse_lanes((17, 8, NZ)), g_ref[:, 2:10, :], g_ref[:, 8:16, :]
        )

    y_even = par_ref[2] == 0

    @pl.when(y_even)
    def _():
        put_high(s1_ref)
        put_low(s2_ref)

    @pl.when(jnp.logical_not(y_even))
    def _():
        put_low(s1_ref)
        put_high(s2_ref)


def finish_kernel(
    par_ref, e_ref, g_ref, r1_ref, r2_ref, h_ref, cell_ref, frac_ref, charge_ref, packed_ref,
    pot_ref, force_ref,
    ee_ref, gg_ref, z_ref, v_ref, o_ref, w_ref, full_ref, turned_ref,
):
    for ref, wide, src in ((ee_ref, 32, e_ref), (gg_ref, 16, g_ref)):
        ref[:, 0:4, :] = jnp.zeros((ref.shape[0], 4, NZ), F32)
        ref[:, 4 + wide :, :] = jnp.zeros((ref.shape[0], 4, NZ), F32)
        ref[:, 4 : 4 + wide, :] = src[...]
    is_coarse = coarse_lanes((17, 5, NZ))

    def merge(low_ref, high_ref):
        ee_ref[:, 0:5, :] += low_ref[0:25, 0:5, :]
        ee_ref[:, 28:33, :] += high_ref[0:25, 0:5, :]
        gg_ref[:, 0:5, :] += low_ref[25:42, 0:5, :]
        high = high_ref[25:42, 0:5, :]
        gg_ref[:, 16:21, :] += jnp.where(is_coarse, 0.0, high)
        gg_ref[:, 10:15, :] += jnp.where(is_coarse, high, 0.0)

    y_even = par_ref[2] == 0

    @pl.when(y_even)
    def _():
        merge(r2_ref, r1_ref)

    @pl.when(jnp.logical_not(y_even))
    def _():
        merge(r1_ref, r2_ref)

    z_ref[...] = dot3(split(ee_ref[...].reshape(1000, NZ)), table(packed_ref, "forward")).reshape(25, 40, 256)
    z_ref[0:17, 0:24, :] += dot3(split(gg_ref[...].reshape(408, NZ)), table(packed_ref, "small")).reshape(
        17, 24, 256
    )
    for group in range(5):
        rows = slice(5 * group, 5 * group + 5)
        both = dot3(table(packed_ref, "line"), split(z_ref[rows].reshape(200, 256)))
        v_ref[rows, :, :NZ] = (both[:200, :NZ] - both[200:, NZ:]).reshape(5, 40, NZ)
        v_ref[rows, :, NZ:] = (both[:200, NZ:] + both[200:, :NZ]).reshape(5, 40, NZ)

    o_ref[CX + 1] = jnp.zeros((40, 256), F32)

    def across(t, carry):
        rows = pl.ds(pl.multiple_of(t * 8, 8), 8)
        for part in range(2):
            acc = [jnp.zeros((8, NZ), F32) for _ in range(CX + 1)]
            for xin in range(CX + KERNEL):
                real = v_ref[xin, rows, :NZ]
                imag = v_ref[xin, rows, NZ:]
                for a in range(KERNEL):
                    x = xin - a
                    if 0 <= x <= CX:
                        h_real = h_ref[a, rows, :NZ]
                        h_imag = h_ref[a, rows, NZ:]
                        if part == 0:
                            acc[x] = acc[x] + real * h_real - imag * h_imag
                        else:
                            acc[x] = acc[x] + real * h_imag + imag * h_real
            for x in range(CX + 1):
                o_ref[x, rows, part * NZ : (part + 1) * NZ] = acc[x]
        return carry

    lax.fori_loop(0, 5, across, 0)
    for group in range(3):
        rows = slice(6 * group, 6 * group + 6)
        both = dot3(table(packed_ref, "back"), split(o_ref[rows].reshape(240, 256)))
        w_ref[rows, :, :NZ] = (both[:192, :NZ] - both[192:, NZ:]).reshape(6, 32, NZ)
        w_ref[rows, :, NZ:] = (both[:192, NZ:] + both[192:, :NZ]).reshape(6, 32, NZ)
    both = dot3(split(w_ref[0:9, 0:16, :].reshape(144, 256)), table(packed_ref, "levels"))
    full = dot3(split(w_ref[0 : CX + 1].reshape((CX + 1) * 32, 256)), table(packed_ref, "inverse"))
    for k, name in enumerate(("plane2", "plane4")):
        full += dot_exact(table(packed_ref, name), both[:, k * NZ : (k + 1) * NZ])
    full_ref[...] = full.reshape(CX + 1, 32, NZ)
    pot_ref[...] = full_ref[0:CX, 0:CY, :]
    for ab in range(4):
        a, b = ab >> 1, ab & 1
        part = full_ref[a : a + CX, b : b + CY, :].reshape(CX * CY, NZ).T
        high, low = split(part)
        turned_ref[ab * NZ : (ab + 1) * NZ, : CX * CY] = high
        turned_ref[ab * NZ : (ab + 1) * NZ, CX * CY :] = low

    def step(t, carry):
        cell, f, charge, span = rows_of(cell_ref, frac_ref, charge_ref, t)
        hot = one_hot(cell)
        hot = jnp.concatenate([hot, hot], axis=0)
        z = cell & (NZ - 1)
        plane = lax.broadcasted_iota(jnp.int32, (NZ, TILE), 0)
        at_low = plane == z
        at_high = plane == ((z + 1) & (NZ - 1))
        corner = []
        for ab in range(4):
            rows = slice(ab * NZ, (ab + 1) * NZ)
            found = jnp.dot(turned_ref[rows, :], hot, preferred_element_type=F32)
            corner.append(
                [
                    jnp.sum(jnp.where(mask, found, 0.0), axis=0, keepdims=True)
                    for mask in (at_low, at_high)
                ]
            )
        wx = [1.0 - f[0], f[0]]
        wy = [1.0 - f[1], f[1]]
        wz = [1.0 - f[2], f[2]]
        sign = [-1.0, 1.0]
        sums = [0.0, 0.0, 0.0]
        for a in range(2):
            for b in range(2):
                for e in range(2):
                    v = corner[2 * a + b][e]
                    sums[0] = sums[0] + sign[a] * wy[b] * wz[e] * v
                    sums[1] = sums[1] + wx[a] * sign[b] * wz[e] * v
                    sums[2] = sums[2] + wx[a] * wy[b] * sign[e] * v
        for k in range(3):
            force_ref[k, 0, :, span] = -charge * sums[k]
        return carry

    lax.fori_loop(0, ATOMS // TILE, step, 0)


def call(kernel, outs, args, spaces, scratch=()):
    return pl.pallas_call(
        kernel,
        out_shape=[jax.ShapeDtypeStruct(shape, F32) for shape in outs],
        in_specs=[pl.BlockSpec(memory_space=space) for space in spaces],
        out_specs=[pl.BlockSpec(memory_space=pltpu.VMEM) for _ in outs],
        scratch_shapes=list(scratch),
        compiler_params=pltpu.CompilerParams(vmem_limit_bytes=VMEM_LIMIT),
    )(*args)


def in_hbm(*values):
    return [pltpu.with_memory_space_constraint(value, pltpu.HBM) for value in values]


def swap(value, axis, first, gap):
    pairs = []
    for i in range(16):
        partner = ((((i - first) % 16) ^ gap) + first) % 16
        pairs.append((i, partner))
    return lax.ppermute(value, axis, pairs)


def per_device(cell, frac, charge, count, fine, middle, coarse):
    packed = jnp.asarray(PACKED)
    ix, iy = lax.axis_index("gx"), lax.axis_index("gy")
    par = jnp.stack([ix & 1, (ix >> 1) & 1, iy & 1]).astype(jnp.int32)
    shat, mc, s1, s2, t1, t2, live = call(
        spread_kernel,
        [(17, 32, NZ), (9, 16, NZ), (5, 48, NZ), (5, 48, NZ), (16, NZ), (16, NZ), (1, 1, ATOMS)],
        (par, count, *in_hbm(cell, frac, charge)),
        [pltpu.SMEM] * 2 + [pltpu.HBM] * 3,
        [
            pltpu.VMEM((1, 1, ATOMS), jnp.int32),
            pltpu.VMEM((3, 1, 1, ATOMS), F32),
            pltpu.VMEM((1, 1, ATOMS), F32),
            pltpu.VMEM((288, (CX + 1) * 32), BF16),
            pltpu.VMEM((CX * CY, 4 * NZ), F32),
            pltpu.SemaphoreType.DMA((3,)),
        ],
    )
    r1 = swap(s1, "gx", 0, 1)
    r2 = swap(s2, "gx", 1, 1)
    rt1 = swap(t1, "gx", 0, 2)
    rt2 = swap(t2, "gx", 2, 2)
    (h,) = call(
        taps_kernel,
        [(KERNEL, 40, 256)],
        (*in_hbm(fine, middle, coarse, packed), live),
        [pltpu.HBM] * 4 + [pl.ANY],
        [
            pltpu.VMEM((KERNEL, KERNEL, KERNEL), F32),
            pltpu.VMEM((KERNEL, KERNEL, KERNEL), F32),
            pltpu.VMEM((KERNEL, KERNEL, KERNEL), F32),
            pltpu.VMEM((PACKED.shape[0] - PLACES["spread_high"][0], 256), BF16),
            pltpu.SemaphoreType.DMA((4,)),
        ],
    )
    e, g, y1, y2 = call(
        merge_kernel,
        [(25, 32, NZ), (17, 16, NZ), (42, 8, NZ), (42, 8, NZ)],
        (par, shat, mc, r1, r2, rt1, rt2, h),
        [pltpu.SMEM] + [pltpu.VMEM] * 6 + [pl.ANY],
    )
    q1 = swap(y1, "gy", 0, 1)
    q2 = swap(y2, "gy", 1, 1)
    pot, force = call(
        finish_kernel,
        [(CX, CY, NZ), (3, 1, 1, ATOMS)],
        (par, e, g, q1, q2, h, cell, frac, live, packed),
        [pltpu.SMEM] + [pltpu.VMEM] * 9,
        [
            pltpu.VMEM((25, 40, NZ), F32),
            pltpu.VMEM((17, 24, NZ), F32),
            pltpu.VMEM((25, 40, 256), F32),
            pltpu.VMEM((25, 40, 256), F32),
            pltpu.VMEM((18, 40, 256), F32),
            pltpu.VMEM((18, 32, 256), F32),
            pltpu.VMEM((CX + 1, 32, NZ), F32),
            pltpu.VMEM((4 * NZ, 2 * CX * CY), BF16),
        ],
    )
    return pot, force


def solution(mesh):
    return jax.shard_map(
        per_device,
        mesh=mesh,
        in_specs=(
            P("gx", "gy", None),
            P(None, "gx", "gy", None),
            P("gx", "gy", None),
            P("gx", "gy"),
            P(),
            P(),
            P(),
        ),
        out_specs=(P("gx", "gy", None), P(None, "gx", "gy", None)),
        check_vma=False,
    )
```

time: 56.6 us -> 43 us (0.76)
  Pallas kernels: 30.1 us -> 22.4 us
  local copies, waits for them, and re-layouts: 3.61 us -> 0.02 us
  waiting for transfers between devices: 8.43 us -> 6.09 us
    pallas_call x4, Pallas kernels: 30.1 us -> 22.4 us  [call(): pl.pallas_call(kernel, out_shape=[jax.ShapeDtypeStruct(shape, F32) for sh...]
    unnamed x26 -> x6, local copies, waits for them, and re-layouts: 3.61 us -> 0.02 us
    ppermute x6, waiting for transfers between devices: 8.43 us -> 6.09 us  [swap(): return lax.ppermute(value, axis, pairs)]
  transfers between devices with their start and end apart: 6 -> 6, of which waited for: 3 -> 2; matrix products, arithmetic and copies ran while one was open for 0% -> 0% of each run, Pallas kernels for 1% -> 7%
where the time goes in v2:
time: 43 us; the launch traced here: 42.8 us
  Pallas kernels  22.4 us (52%)
  starting transfers between devices  12.7 us (30%)
  waiting for transfers between devices  6.09 us (14%)
  between operations  1.5 us (3%)
    pallas_call x4, Pallas kernels, call(): pl.pallas_call(kernel, out_shape=[jax.ShapeDtypeStruct(shape, F32) for sh...  22.4 us
    ppermute x6, starting transfers between devices, swap(): return lax.ppermute(value, axis, pairs)  12.7 us
    ppermute x6, waiting for transfers between devices, swap(): return lax.ppermute(value, axis, pairs)  6.09 us
  transfers between devices with their start and end apart: 6, of which 2 were waited for; matrix products, arithmetic and copies ran while one was open for 0% of the time, Pallas kernels for 7%

profile of v2, /device:TPU:4, one launch (start us, length us, event | category | flops | bytes accessed | tf_op | source)
XLA Modules:
  0.0 42.8 jit_solution(15167651130389451810)
XLA Ops:
  0.6 0.0 copy-start
  0.6 0.0 copy-start.1
  0.7 0.0 copy-start.2
  1.5 0.1 pad_add_fusion.par_ref
  1.5 7.1 %shard_map.95 = (f32[17,32,128]{2,1,0:T(8,128)S(1)}, f32[9,16,128]{2,1,0:T(8,128)S(1)}, f32[5,48,128]{2,1,0:T(8,128)S(1)}, f32[5,48,128]{2,1,0:T(8,128)S(1)}, f3...) custom-call(s32[3]{0:T(128)S(1)} %pad_add_fusion.par_ref, s32[1,1]{1,0:T(1,128)S(6)} %copy.10.count_ref, ...), custom_call_target="tpu_custom_call" | custom-call | tf_op jit(solution)/shard_map/pallas_call | solution.py:540
  8.6 1.3 %collective-permute-start = (f32[5,48,128]{2,1,0:T(8,128)S(1)}, f32[5,48,128]{2,1,0:T(8,128)S(1)}, u32[]{:S(2)}, u32[]{:S(2)}) collective-permute-start(f32[5,48,128]{2,1,0:T(8,128)S(1)} %get-tuple-element.15), channel_id=1, source_target_pairs={{0,16},{16,0},{32,48},{48,32},{64,80},{80,64},{96,112},{112,96},{1... | collective-permute-start | bytes 368648 | tf_op jit(solution)/shard_map/ppermute | solution.py:559
  9.9 1.6 %collective-permute-start.1 = (f32[5,48,128]{2,1,0:T(8,128)S(1)}, f32[5,48,128]{2,1,0:T(8,128)S(1)}, u32[]{:S(2)}, u32[]{:S(2)}) collective-permute-start(f32[5,48,128]{2,1,0:T(8,128)S(1)} %get-tuple-element.16), channel_id=1, source_target_pairs={{0,240},{16,32},{32,16},{48,64},{64,48},{80,96},{96,80},{112,128},... | collective-permute-start | bytes 368648 | tf_op jit(solution)/shard_map/ppermute | solution.py:559
  11.5 3.7 %collective-permute-start.2 = (f32[16,128]{1,0:T(8,128)S(1)}, f32[16,128]{1,0:T(8,128)S(1)}, u32[]{:S(2)}, u32[]{:S(2)}) collective-permute-start(f32[16,128]{1,0:T(8,128)S(1)} %get-tuple-element.17), channel_id=1, source_target_pairs={{0,32},{16,48},{32,0},{48,16},{64,96},{80,112},{96,64},{112,80},{1... | collective-permute-start | bytes 24584 | tf_op jit(solution)/shard_map/ppermute | solution.py:559
  15.3 0.0 collective-permute-start.3
  15.3 3.0 %shard_map.96.h_ref = f32[9,40,256]{2,1,0:T(8,128)S(1)} custom-call(f32[9,9,9]{2,1,0:T(8,128)} %fine_hbm.1, f32[9,9,9]{2,1,0:T(8,128)} %middle_hbm.1, f32[9,9,9]{2,1,0:T(8,128)} %coarse_hbm.1, bf16[4448,256]{1,0:T(8,128)(2,1)} %constant.11.clone.packed_hbm.packed_ref, f32[1,1,4096]{2,1,0:T(1,128)S(1)} %get-tuple-element.19.live_ref.charge_ref), custom_call_target="tpu_custom_call" | custom-call | tf_op jit(solution)/shard_map/pallas_call | solution.py:540
  18.3 0.0 collective-permute-done.2.rt1_ref
  18.3 3.0 %collective-permute-done.3.rt2_ref = f32[16,128]{1,0:T(8,128)S(1)} collective-permute-done((f32[16,128]{1,0:T(8,128)S(1)}, f32[16,128]{1,0:T(8,128)S(1)}, u32[]{:S(2)}, u32[]{:S(2)}) %collective-permute-start.3) | collective-permute-done | bytes 8224 | tf_op jit(solution)/shard_map/ppermute | solution.py:559
  21.3 0.0 collective-permute-done.r1_ref
  21.3 0.0 collective-permute-done.1.r2_ref
  21.3 0.7 %shard_map.97 = (f32[25,32,128]{2,1,0:T(8,128)S(1)}, f32[17,16,128]{2,1,0:T(8,128)S(1)}, f32[42,8,128]{2,1,0:T(8,128)S(1)}, f32[42,8,128]{2,1,0:T(8,128)S(1)}) custom-call(s32[3]{0:T(128)S(1)} %pad_add_fusion.par_ref, f32[17,32,128]{2,1,0:T(8,128)S(1)} %get-tuple-element.13.shat_ref, f32[9,16,128]{2,1,0:T(8,128)S(1)} %get-tuple-element.14.mc_ref, ...), custom_call_target="tpu_custom_call" | custom-call | tf_op jit(solution)/shard_map/pallas_call | solution.py:540
  22.0 0.1 collective-permute-start.4
  22.1 6.0 %collective-permute-start.5 = (f32[42,8,128]{2,1,0:T(8,128)S(1)}, f32[42,8,128]{2,1,0:T(8,128)S(1)}, u32[]{:S(2)}, u32[]{:S(2)}) collective-permute-start(f32[42,8,128]{2,1,0:T(8,128)S(1)} %get-tuple-element.23), channel_id=1, source_target_pairs={{0,15},{1,2},{2,1},{3,4},{4,3},{5,6},{6,5},{7,8},{8,7},{9,10},{10,... | collective-permute-start | bytes 516104 | tf_op jit(solution)/shard_map/ppermute | solution.py:559
  28.1 0.0 collective-permute-done.4.r1_ref
  28.1 3.1 %collective-permute-done.5.r2_ref = f32[42,8,128]{2,1,0:T(8,128)S(1)} collective-permute-done((f32[42,8,128]{2,1,0:T(8,128)S(1)}, f32[42,8,128]{2,1,0:T(8,128)S(1)}, u32[]{:S(2)}, u32[]{:S(2)}) %collective-permute-start.5) | collective-permute-done | bytes 172064 | tf_op jit(solution)/shard_map/ppermute | solution.py:559
  31.2 0.0 copy-done
  31.2 0.0 copy-done.1
  31.2 0.0 copy-done.2
  31.2 11.6 %shard_map.98 = (f32[16,24,128]{2,1,0:T(8,128)}, f32[3,1,1,4096]{3,2,1,0:T(1,128)}) custom-call(s32[3]{0:T(128)S(1)} %pad_add_fusion.par_ref, f32[25,32,128]{2,1,0:T(8,128)S(1)} %get-tuple-element.20.e_ref, f32[17,16,128]{2,1,0:T(8,128)S(1)} %get-tuple-element.21.g_ref, f32[42,8,128]{2,1,0:T(8,128)S(1)} %collective-permute-done.4.r1_ref, ...), custom_call_target="tpu_custom_call" | custom-call | tf_op jit(solution)/shard_map/pallas_call | solution.py:540
Async XLA Ops:
  0.6 30.5 %copy-start = (bf16[4448,256]{1,0:T(8,128)(2,1)S(1)}, bf16[4448,256]{1,0:T(8,128)(2,1)}, u32[]{:S(2)}) copy-start(bf16[4448,256]{1,0:T(8,128)(2,1)} %constant.11.clone.packed_hbm.packed_ref) | copy-start | bytes 6832132
  0.6 30.5 %copy-start.1 = (f32[3,1,1,4096]{3,2,1,0:T(1,128)S(1)}, f32[3,1,1,4096]{3,2,1,0:T(1,128)}, u32[]{:S(2)}) copy-start(f32[3,1,1,4096]{3,2,1,0:T(1,128)} %frac_ref.1) | copy-start | bytes 147460
  0.7 30.5 %copy-start.2 = (s32[1,1,4096]{2,1,0:T(1,128)S(1)}, s32[1,1,4096]{2,1,0:T(1,128)}, u32[]{:S(2)}) copy-start(s32[1,1,4096]{2,1,0:T(1,128)} %cell_ref.1) | copy-start | bytes 49156
  8.6 12.7 %collective-permute-start = (f32[5,48,128]{2,1,0:T(8,128)S(1)}, f32[5,48,128]{2,1,0:T(8,128)S(1)}, u32[]{:S(2)}, u32[]{:S(2)}) collective-permute-start(f32[5,48,128]{2,1,0:T(8,128)S(1)} %get-tuple-element.15), channel_id=1, source_target_pairs={{0,16},{16,0},{32,48},{48,32},{64,80},{80,64},{96,112},{112,96},{1... | collective-permute-start | bytes 368648 | tf_op jit(solution)/shard_map/ppermute | solution.py:559
  9.9 11.4 %collective-permute-start.1 = (f32[5,48,128]{2,1,0:T(8,128)S(1)}, f32[5,48,128]{2,1,0:T(8,128)S(1)}, u32[]{:S(2)}, u32[]{:S(2)}) collective-permute-start(f32[5,48,128]{2,1,0:T(8,128)S(1)} %get-tuple-element.16), channel_id=1, source_target_pairs={{0,240},{16,32},{32,16},{48,64},{64,48},{80,96},{96,80},{112,128},... | collective-permute-start | bytes 368648 | tf_op jit(solution)/shard_map/ppermute | solution.py:559
  11.5 6.8 %collective-permute-start.2 = (f32[16,128]{1,0:T(8,128)S(1)}, f32[16,128]{1,0:T(8,128)S(1)}, u32[]{:S(2)}, u32[]{:S(2)}) collective-permute-start(f32[16,128]{1,0:T(8,128)S(1)} %get-tuple-element.17), channel_id=1, source_target_pairs={{0,32},{16,48},{32,0},{48,16},{64,96},{80,112},{96,64},{112,80},{1... | collective-permute-start | bytes 24584 | tf_op jit(solution)/shard_map/ppermute | solution.py:559
  15.3 6.1 %collective-permute-start.3 = (f32[16,128]{1,0:T(8,128)S(1)}, f32[16,128]{1,0:T(8,128)S(1)}, u32[]{:S(2)}, u32[]{:S(2)}) collective-permute-start(f32[16,128]{1,0:T(8,128)S(1)} %get-tuple-element.18), channel_id=1, source_target_pairs={{0,224},{16,240},{32,64},{48,80},{64,32},{80,48},{96,128},{112,144... | collective-permute-start | bytes 24584 | tf_op jit(solution)/shard_map/ppermute | solution.py:559
  22.0 6.1 %collective-permute-start.4 = (f32[42,8,128]{2,1,0:T(8,128)S(1)}, f32[42,8,128]{2,1,0:T(8,128)S(1)}, u32[]{:S(2)}, u32[]{:S(2)}) collective-permute-start(f32[42,8,128]{2,1,0:T(8,128)S(1)} %get-tuple-element.22), channel_id=1, source_target_pairs={{0,1},{1,0},{2,3},{3,2},{4,5},{5,4},{6,7},{7,6},{8,9},{9,8},{10,11... | collective-permute-start | bytes 516104 | tf_op jit(solution)/shard_map/ppermute | solution.py:559
  22.1 9.0 %collective-permute-start.5 = (f32[42,8,128]{2,1,0:T(8,128)S(1)}, f32[42,8,128]{2,1,0:T(8,128)S(1)}, u32[]{:S(2)}, u32[]{:S(2)}) collective-permute-start(f32[42,8,128]{2,1,0:T(8,128)S(1)} %get-tuple-element.23), channel_id=1, source_target_pairs={{0,15},{1,2},{2,1},{3,4},{4,3},{5,6},{6,5},{7,8},{8,7},{9,10},{10,... | collective-permute-start | bytes 516104 | tf_op jit(solution)/shard_map/ppermute | solution.py:559

commit v3 on v2

--- a/solution.py
+++ b/solution.py
@@ -257,6 +257,8 @@
         wx = [1.0 - f[0], f[0]]
         wy = [1.0 - f[1], f[1]]
         wz = [1.0 - f[2], f[2]]
+        low_hot = jnp.where(at_low, 1.0, 0.0).astype(BF16)
+        high_hot = jnp.where(at_high, 1.0, 0.0).astype(BF16)
         highs = []
         lows = []
         for ab in range(4):
@@ -267,9 +269,7 @@
                 (highs, tops),
                 (lows, [w - t for w, t in zip(weights, tops)]),
             ):
-                group.append(
-                    jnp.where(at_low, w0, jnp.where(at_high, w1, 0.0)).astype(BF16)
-                )
+                group.append(low_hot * w0.astype(BF16) + high_hot * w1.astype(BF16))
         dims = (((1,), (1,)), ((), ()))
         acc_ref[...] += sum(
             lax.dot_general(
@@ -279,7 +279,7 @@
         )
         return carry
 
-    lax.fori_loop(0, ATOMS // TILE, step, 0)
+    lax.fori_loop(0, ATOMS // TILE, step, 0, unroll=True)
     for ab in range(4):
         a, b = ab >> 1, ab & 1
         for x in range(CX):

time: 43 us -> 41.8 us (0.972)
  Pallas kernels: 22.4 us -> 21.2 us
    pallas_call x4, Pallas kernels: 22.4 us -> 21.2 us  [call(): pl.pallas_call(kernel, out_shape=[jax.ShapeDtypeStruct(shape, F32) for sh...]
where the time goes in v3:
time: 41.8 us; the launch traced here: 41.6 us
  Pallas kernels  21.2 us (51%)
  starting transfers between devices  12.7 us (30%)
  waiting for transfers between devices  6.09 us (15%)
  between operations  1.51 us (4%)
    pallas_call x4, Pallas kernels, call(): pl.pallas_call(kernel, out_shape=[jax.ShapeDtypeStruct(shape, F32) for sh...  21.2 us
    ppermute x6, starting transfers between devices, swap(): return lax.ppermute(value, axis, pairs)  12.7 us
    ppermute x6, waiting for transfers between devices, swap(): return lax.ppermute(value, axis, pairs)  6.09 us
  transfers between devices with their start and end apart: 6, of which 2 were waited for; matrix products, arithmetic and copies ran while one was open for 0% of the time, Pallas kernels for 7%

profile of v3, /device:TPU:4, one launch (start us, length us, event | category | flops | bytes accessed | tf_op | source)
XLA Modules:
  0.0 41.6 jit_solution(4834540116044257568)
XLA Ops:
  0.6 0.0 copy-start
  0.6 0.0 copy-start.1
  0.7 0.0 copy-start.2
  1.5 0.1 pad_add_fusion.par_ref
  1.5 5.7 %shard_map.95 = (f32[17,32,128]{2,1,0:T(8,128)S(1)}, f32[9,16,128]{2,1,0:T(8,128)S(1)}, f32[5,48,128]{2,1,0:T(8,128)S(1)}, f32[5,48,128]{2,1,0:T(8,128)S(1)}, f3...) custom-call(s32[3]{0:T(128)S(1)} %pad_add_fusion.par_ref, s32[1,1]{1,0:T(1,128)S(6)} %copy.10.count_ref, ...), custom_call_target="tpu_custom_call" | custom-call | tf_op jit(solution)/shard_map/pallas_call | solution.py:540
  7.3 1.3 %collective-permute-start = (f32[5,48,128]{2,1,0:T(8,128)S(1)}, f32[5,48,128]{2,1,0:T(8,128)S(1)}, u32[]{:S(2)}, u32[]{:S(2)}) collective-permute-start(f32[5,48,128]{2,1,0:T(8,128)S(1)} %get-tuple-element.15), channel_id=1, source_target_pairs={{0,16},{16,0},{32,48},{48,32},{64,80},{80,64},{96,112},{112,96},{1... | collective-permute-start | bytes 368648 | tf_op jit(solution)/shard_map/ppermute | solution.py:559
  8.6 1.6 %collective-permute-start.1 = (f32[5,48,128]{2,1,0:T(8,128)S(1)}, f32[5,48,128]{2,1,0:T(8,128)S(1)}, u32[]{:S(2)}, u32[]{:S(2)}) collective-permute-start(f32[5,48,128]{2,1,0:T(8,128)S(1)} %get-tuple-element.16), channel_id=1, source_target_pairs={{0,240},{16,32},{32,16},{48,64},{64,48},{80,96},{96,80},{112,128},... | collective-permute-start | bytes 368648 | tf_op jit(solution)/shard_map/ppermute | solution.py:559
  10.2 3.7 %collective-permute-start.2 = (f32[16,128]{1,0:T(8,128)S(1)}, f32[16,128]{1,0:T(8,128)S(1)}, u32[]{:S(2)}, u32[]{:S(2)}) collective-permute-start(f32[16,128]{1,0:T(8,128)S(1)} %get-tuple-element.17), channel_id=1, source_target_pairs={{0,32},{16,48},{32,0},{48,16},{64,96},{80,112},{96,64},{112,80},{1... | collective-permute-start | bytes 24584 | tf_op jit(solution)/shard_map/ppermute | solution.py:559
  13.9 0.0 collective-permute-start.3
  13.9 3.0 %shard_map.96.h_ref = f32[9,40,256]{2,1,0:T(8,128)S(1)} custom-call(f32[9,9,9]{2,1,0:T(8,128)} %fine_hbm.1, f32[9,9,9]{2,1,0:T(8,128)} %middle_hbm.1, f32[9,9,9]{2,1,0:T(8,128)} %coarse_hbm.1, bf16[4448,256]{1,0:T(8,128)(2,1)} %constant.11.clone.packed_hbm.packed_ref, f32[1,1,4096]{2,1,0:T(1,128)S(1)} %get-tuple-element.19.live_ref.charge_ref), custom_call_target="tpu_custom_call" | custom-call | tf_op jit(solution)/shard_map/pallas_call | solution.py:540
  17.0 0.0 collective-permute-done.2.rt1_ref
  17.0 3.0 %collective-permute-done.3.rt2_ref = f32[16,128]{1,0:T(8,128)S(1)} collective-permute-done((f32[16,128]{1,0:T(8,128)S(1)}, f32[16,128]{1,0:T(8,128)S(1)}, u32[]{:S(2)}, u32[]{:S(2)}) %collective-permute-start.3) | collective-permute-done | bytes 8224 | tf_op jit(solution)/shard_map/ppermute | solution.py:559
  20.0 0.0 collective-permute-done.r1_ref
  20.0 0.0 collective-permute-done.1.r2_ref
  20.0 0.7 %shard_map.97 = (f32[25,32,128]{2,1,0:T(8,128)S(1)}, f32[17,16,128]{2,1,0:T(8,128)S(1)}, f32[42,8,128]{2,1,0:T(8,128)S(1)}, f32[42,8,128]{2,1,0:T(8,128)S(1)}) custom-call(s32[3]{0:T(128)S(1)} %pad_add_fusion.par_ref, f32[17,32,128]{2,1,0:T(8,128)S(1)} %get-tuple-element.13.shat_ref, f32[9,16,128]{2,1,0:T(8,128)S(1)} %get-tuple-element.14.mc_ref, ...), custom_call_target="tpu_custom_call" | custom-call | tf_op jit(solution)/shard_map/pallas_call | solution.py:540
  20.6 0.1 collective-permute-start.4
  20.7 6.0 %collective-permute-start.5 = (f32[42,8,128]{2,1,0:T(8,128)S(1)}, f32[42,8,128]{2,1,0:T(8,128)S(1)}, u32[]{:S(2)}, u32[]{:S(2)}) collective-permute-start(f32[42,8,128]{2,1,0:T(8,128)S(1)} %get-tuple-element.23), channel_id=1, source_target_pairs={{0,15},{1,2},{2,1},{3,4},{4,3},{5,6},{6,5},{7,8},{8,7},{9,10},{10,... | collective-permute-start | bytes 516104 | tf_op jit(solution)/shard_map/ppermute | solution.py:559
  26.7 0.0 collective-permute-done.4.r1_ref
  26.7 3.1 %collective-permute-done.5.r2_ref = f32[42,8,128]{2,1,0:T(8,128)S(1)} collective-permute-done((f32[42,8,128]{2,1,0:T(8,128)S(1)}, f32[42,8,128]{2,1,0:T(8,128)S(1)}, u32[]{:S(2)}, u32[]{:S(2)}) %collective-permute-start.5) | collective-permute-done | bytes 172064 | tf_op jit(solution)/shard_map/ppermute | solution.py:559
  29.8 0.0 copy-done
  29.8 0.0 copy-done.1
  29.8 0.0 copy-done.2
  29.8 11.8 %shard_map.98 = (f32[16,24,128]{2,1,0:T(8,128)}, f32[3,1,1,4096]{3,2,1,0:T(1,128)}) custom-call(s32[3]{0:T(128)S(1)} %pad_add_fusion.par_ref, f32[25,32,128]{2,1,0:T(8,128)S(1)} %get-tuple-element.20.e_ref, f32[17,16,128]{2,1,0:T(8,128)S(1)} %get-tuple-element.21.g_ref, f32[42,8,128]{2,1,0:T(8,128)S(1)} %collective-permute-done.4.r1_ref, ...), custom_call_target="tpu_custom_call" | custom-call | tf_op jit(solution)/shard_map/pallas_call | solution.py:540
Async XLA Ops:
  0.6 29.2 %copy-start = (bf16[4448,256]{1,0:T(8,128)(2,1)S(1)}, bf16[4448,256]{1,0:T(8,128)(2,1)}, u32[]{:S(2)}) copy-start(bf16[4448,256]{1,0:T(8,128)(2,1)} %constant.11.clone.packed_hbm.packed_ref) | copy-start | bytes 6832132
  0.6 29.2 %copy-start.1 = (f32[3,1,1,4096]{3,2,1,0:T(1,128)S(1)}, f32[3,1,1,4096]{3,2,1,0:T(1,128)}, u32[]{:S(2)}) copy-start(f32[3,1,1,4096]{3,2,1,0:T(1,128)} %frac_ref.1) | copy-start | bytes 147460
  0.7 29.1 %copy-start.2 = (s32[1,1,4096]{2,1,0:T(1,128)S(1)}, s32[1,1,4096]{2,1,0:T(1,128)}, u32[]{:S(2)}) copy-start(s32[1,1,4096]{2,1,0:T(1,128)} %cell_ref.1) | copy-start | bytes 49156
  7.3 12.7 %collective-permute-start = (f32[5,48,128]{2,1,0:T(8,128)S(1)}, f32[5,48,128]{2,1,0:T(8,128)S(1)}, u32[]{:S(2)}, u32[]{:S(2)}) collective-permute-start(f32[5,48,128]{2,1,0:T(8,128)S(1)} %get-tuple-element.15), channel_id=1, source_target_pairs={{0,16},{16,0},{32,48},{48,32},{64,80},{80,64},{96,112},{112,96},{1... | collective-permute-start | bytes 368648 | tf_op jit(solution)/shard_map/ppermute | solution.py:559
  8.6 11.4 %collective-permute-start.1 = (f32[5,48,128]{2,1,0:T(8,128)S(1)}, f32[5,48,128]{2,1,0:T(8,128)S(1)}, u32[]{:S(2)}, u32[]{:S(2)}) collective-permute-start(f32[5,48,128]{2,1,0:T(8,128)S(1)} %get-tuple-element.16), channel_id=1, source_target_pairs={{0,240},{16,32},{32,16},{48,64},{64,48},{80,96},{96,80},{112,128},... | collective-permute-start | bytes 368648 | tf_op jit(solution)/shard_map/ppermute | solution.py:559
  10.2 6.8 %collective-permute-start.2 = (f32[16,128]{1,0:T(8,128)S(1)}, f32[16,128]{1,0:T(8,128)S(1)}, u32[]{:S(2)}, u32[]{:S(2)}) collective-permute-start(f32[16,128]{1,0:T(8,128)S(1)} %get-tuple-element.17), channel_id=1, source_target_pairs={{0,32},{16,48},{32,0},{48,16},{64,96},{80,112},{96,64},{112,80},{1... | collective-permute-start | bytes 24584 | tf_op jit(solution)/shard_map/ppermute | solution.py:559
  13.9 6.1 %collective-permute-start.3 = (f32[16,128]{1,0:T(8,128)S(1)}, f32[16,128]{1,0:T(8,128)S(1)}, u32[]{:S(2)}, u32[]{:S(2)}) collective-permute-start(f32[16,128]{1,0:T(8,128)S(1)} %get-tuple-element.18), channel_id=1, source_target_pairs={{0,224},{16,240},{32,64},{48,80},{64,32},{80,48},{96,128},{112,144... | collective-permute-start | bytes 24584 | tf_op jit(solution)/shard_map/ppermute | solution.py:559
  20.6 6.1 %collective-permute-start.4 = (f32[42,8,128]{2,1,0:T(8,128)S(1)}, f32[42,8,128]{2,1,0:T(8,128)S(1)}, u32[]{:S(2)}, u32[]{:S(2)}) collective-permute-start(f32[42,8,128]{2,1,0:T(8,128)S(1)} %get-tuple-element.22), channel_id=1, source_target_pairs={{0,1},{1,0},{2,3},{3,2},{4,5},{5,4},{6,7},{7,6},{8,9},{9,8},{10,11... | collective-permute-start | bytes 516104 | tf_op jit(solution)/shard_map/ppermute | solution.py:559
  20.7 9.0 %collective-permute-start.5 = (f32[42,8,128]{2,1,0:T(8,128)S(1)}, f32[42,8,128]{2,1,0:T(8,128)S(1)}, u32[]{:S(2)}, u32[]{:S(2)}) collective-permute-start(f32[42,8,128]{2,1,0:T(8,128)S(1)} %get-tuple-element.23), channel_id=1, source_target_pairs={{0,15},{1,2},{2,1},{3,4},{4,3},{5,6},{6,5},{7,8},{8,7},{9,10},{10,... | collective-permute-start | bytes 516104 | tf_op jit(solution)/shard_map/ppermute | solution.py:559

commit v4 on v3

--- a/solution.py
+++ b/solution.py
@@ -17,7 +17,7 @@
 HIGHEST = lax.Precision.HIGHEST
 F32 = jnp.float32
 BF16 = jnp.bfloat16
-VMEM_LIMIT = 48 * 1024 * 1024
+VMEM_LIMIT = 28 * 1024 * 1024
 
 
 LINE = CY + KERNEL
@@ -419,8 +419,17 @@
         put_high(s2_ref)
 
 
+def hot_kernel(cell_ref, e_ref, hot_ref):
+    def step(t, carry):
+        span = pl.ds(pl.multiple_of(t * TILE, TILE), TILE)
+        hot_ref[:, span] = one_hot(cell_ref[0, :, span])
+        return carry
+
+    lax.fori_loop(0, ATOMS // TILE, step, 0)
+
+
 def finish_kernel(
-    par_ref, e_ref, g_ref, r1_ref, r2_ref, h_ref, cell_ref, frac_ref, charge_ref, packed_ref,
+    par_ref, e_ref, g_ref, r1_ref, r2_ref, h_ref, hot_ref, cell_ref, frac_ref, charge_ref, packed_ref,
     pot_ref, force_ref,
     ee_ref, gg_ref, z_ref, v_ref, o_ref, w_ref, full_ref, turned_ref,
 ):
@@ -501,7 +510,7 @@
 
     def step(t, carry):
         cell, f, charge, span = rows_of(cell_ref, frac_ref, charge_ref, t)
-        hot = one_hot(cell)
+        hot = hot_ref[:, span]
         hot = jnp.concatenate([hot, hot], axis=0)
         z = cell & (NZ - 1)
         plane = lax.broadcasted_iota(jnp.int32, (NZ, TILE), 0)
@@ -536,10 +545,10 @@
     lax.fori_loop(0, ATOMS // TILE, step, 0)
 
 
-def call(kernel, outs, args, spaces, scratch=()):
+def call(kernel, outs, args, spaces, scratch=(), dtype=F32):
     return pl.pallas_call(
         kernel,
-        out_shape=[jax.ShapeDtypeStruct(shape, F32) for shape in outs],
+        out_shape=[jax.ShapeDtypeStruct(shape, dtype) for shape in outs],
         in_specs=[pl.BlockSpec(memory_space=space) for space in spaces],
         out_specs=[pl.BlockSpec(memory_space=pltpu.VMEM) for _ in outs],
         scratch_shapes=list(scratch),
@@ -602,11 +611,14 @@
     )
     q1 = swap(y1, "gy", 0, 1)
     q2 = swap(y2, "gy", 1, 1)
+    (hot,) = call(
+        hot_kernel, [(CX * CY, ATOMS)], (cell, e), [pltpu.VMEM, pl.ANY], dtype=BF16
+    )
     pot, force = call(
         finish_kernel,
         [(CX, CY, NZ), (3, 1, 1, ATOMS)],
-        (par, e, g, q1, q2, h, cell, frac, live, packed),
-        [pltpu.SMEM] + [pltpu.VMEM] * 9,
+        (par, e, g, q1, q2, h, hot, cell, frac, live, packed),
+        [pltpu.SMEM] + [pltpu.VMEM] * 10,
         [
             pltpu.VMEM((25, 40, NZ), F32),
             pltpu.VMEM((17, 24, NZ), F32),

time: 41.8 us -> 41.3 us (0.988)
  waiting for transfers between devices: 6.09 us -> 5.39 us
    ppermute x6, waiting for transfers between devices: 6.09 us -> 5.39 us  [swap(): return lax.ppermute(value, axis, pairs)]
    pallas_call x4 -> x5, Pallas kernels: 21.2 us -> 21.5 us  [call(): pl.pallas_call(kernel, out_shape=[jax.ShapeDtypeStruct(shape, dtype) for...]
  transfers between devices with their start and end apart: 6 -> 6, of which waited for: 2 -> 2; matrix products, arithmetic and copies ran while one was open for 0% -> 0% of each run, Pallas kernels for 7% -> 9%
where the time goes in v4:
time: 41.3 us; the launch traced here: 41 us
  Pallas kernels  21.5 us (52%)
  starting transfers between devices  12.7 us (31%)
  waiting for transfers between devices  5.39 us (13%)
  between operations  1.36 us (3%)
    pallas_call x5, Pallas kernels, call(): pl.pallas_call(kernel, out_shape=[jax.ShapeDtypeStruct(shape, dtype) for...  21.5 us
    ppermute x6, starting transfers between devices, swap(): return lax.ppermute(value, axis, pairs)  12.7 us
    ppermute x6, waiting for transfers between devices, swap(): return lax.ppermute(value, axis, pairs)  5.39 us
  transfers between devices with their start and end apart: 6, of which 2 were waited for; matrix products, arithmetic and copies ran while one was open for 0% of the time, Pallas kernels for 9%

profile of v4, /device:TPU:4, one launch (start us, length us, event | category | flops | bytes accessed | tf_op | source)
XLA Modules:
  0.0 41.0 jit_solution(10501739217831029908)
XLA Ops:
  0.6 0.0 copy-start.2
  1.3 0.1 pad_add_fusion.par_ref
  1.4 5.7 %shard_map.95 = (f32[17,32,128]{2,1,0:T(8,128)S(1)}, f32[9,16,128]{2,1,0:T(8,128)S(1)}, f32[5,48,128]{2,1,0:T(8,128)S(1)}, f32[5,48,128]{2,1,0:T(8,128)S(1)}, f3...) custom-call(s32[3]{0:T(128)S(1)} %pad_add_fusion.par_ref, s32[1,1]{1,0:T(1,128)S(6)} %copy.10.count_ref, ...), custom_call_target="tpu_custom_call" | custom-call | tf_op jit(solution)/shard_map/pallas_call | solution.py:549
  7.1 1.3 %collective-permute-start = (f32[5,48,128]{2,1,0:T(8,128)S(1)}, f32[5,48,128]{2,1,0:T(8,128)S(1)}, u32[]{:S(2)}, u32[]{:S(2)}) collective-permute-start(f32[5,48,128]{2,1,0:T(8,128)S(1)} %get-tuple-element.15), channel_id=1, source_target_pairs={{0,16},{16,0},{32,48},{48,32},{64,80},{80,64},{96,112},{112,96},{1... | collective-permute-start | bytes 368648 | tf_op jit(solution)/shard_map/ppermute | solution.py:568
  8.4 1.6 %collective-permute-start.1 = (f32[5,48,128]{2,1,0:T(8,128)S(1)}, f32[5,48,128]{2,1,0:T(8,128)S(1)}, u32[]{:S(2)}, u32[]{:S(2)}) collective-permute-start(f32[5,48,128]{2,1,0:T(8,128)S(1)} %get-tuple-element.16), channel_id=1, source_target_pairs={{0,240},{16,32},{32,16},{48,64},{64,48},{80,96},{96,80},{112,128},... | collective-permute-start | bytes 368648 | tf_op jit(solution)/shard_map/ppermute | solution.py:568
  10.0 3.7 %collective-permute-start.2 = (f32[16,128]{1,0:T(8,128)S(1)}, f32[16,128]{1,0:T(8,128)S(1)}, u32[]{:S(2)}, u32[]{:S(2)}) collective-permute-start(f32[16,128]{1,0:T(8,128)S(1)} %get-tuple-element.17), channel_id=1, source_target_pairs={{0,32},{16,48},{32,0},{48,16},{64,96},{80,112},{96,64},{112,80},{1... | collective-permute-start | bytes 24584 | tf_op jit(solution)/shard_map/ppermute | solution.py:568
  13.7 0.0 collective-permute-start.3
  13.7 0.0 copy-start
  13.7 0.0 copy-start.1
  13.7 3.2 %shard_map.96.h_ref = f32[9,40,256]{2,1,0:T(8,128)S(1)} custom-call(f32[9,9,9]{2,1,0:T(8,128)} %fine_hbm.1, f32[9,9,9]{2,1,0:T(8,128)} %middle_hbm.1, f32[9,9,9]{2,1,0:T(8,128)} %coarse_hbm.1, bf16[4448,256]{1,0:T(8,128)(2,1)} %constant.11.clone.packed_hbm.packed_ref, f32[1,1,4096]{2,1,0:T(1,128)S(1)} %get-tuple-element.19.live_ref.charge_ref), custom_call_target="tpu_custom_call" | custom-call | tf_op jit(solution)/shard_map/pallas_call | solution.py:549
  16.9 0.0 collective-permute-done.2.rt1_ref
  16.9 2.9 %collective-permute-done.3.rt2_ref = f32[16,128]{1,0:T(8,128)S(1)} collective-permute-done((f32[16,128]{1,0:T(8,128)S(1)}, f32[16,128]{1,0:T(8,128)S(1)}, u32[]{:S(2)}, u32[]{:S(2)}) %collective-permute-start.3) | collective-permute-done | bytes 8224 | tf_op jit(solution)/shard_map/ppermute | solution.py:568
  19.8 0.0 collective-permute-done.r1_ref
  19.8 0.0 collective-permute-done.1.r2_ref
  19.8 0.7 %shard_map.97 = (f32[25,32,128]{2,1,0:T(8,128)S(1)}, f32[17,16,128]{2,1,0:T(8,128)S(1)}, f32[42,8,128]{2,1,0:T(8,128)S(1)}, f32[42,8,128]{2,1,0:T(8,128)S(1)}) custom-call(s32[3]{0:T(128)S(1)} %pad_add_fusion.par_ref, f32[17,32,128]{2,1,0:T(8,128)S(1)} %get-tuple-element.13.shat_ref, f32[9,16,128]{2,1,0:T(8,128)S(1)} %get-tuple-element.14.mc_ref, ...), custom_call_target="tpu_custom_call" | custom-call | tf_op jit(solution)/shard_map/pallas_call | solution.py:549
  20.5 0.1 collective-permute-start.4
  20.6 6.0 %collective-permute-start.5 = (f32[42,8,128]{2,1,0:T(8,128)S(1)}, f32[42,8,128]{2,1,0:T(8,128)S(1)}, u32[]{:S(2)}, u32[]{:S(2)}) collective-permute-start(f32[42,8,128]{2,1,0:T(8,128)S(1)} %get-tuple-element.23), channel_id=1, source_target_pairs={{0,15},{1,2},{2,1},{3,4},{4,3},{5,6},{6,5},{7,8},{8,7},{9,10},{10,... | collective-permute-start | bytes 516104 | tf_op jit(solution)/shard_map/ppermute | solution.py:568
  26.5 0.0 copy-done.2
  26.5 0.6 %shard_map.98.hot_ref = bf16[384,4096]{1,0:T(8,128)(2,1)S(1)} custom-call(s32[1,1,4096]{2,1,0:T(1,128)S(1)} %copy-done.2, f32[25,32,128]{2,1,0:T(8,128)S(1)} %get-tuple-element.20.e_ref), custom_call_target="tpu_custom_call" | custom-call | tf_op jit(solution)/shard_map/pallas_call | solution.py:549
  27.1 0.0 collective-permute-done.4.r1_ref
  27.1 2.5 %collective-permute-done.5.r2_ref = f32[42,8,128]{2,1,0:T(8,128)S(1)} collective-permute-done((f32[42,8,128]{2,1,0:T(8,128)S(1)}, f32[42,8,128]{2,1,0:T(8,128)S(1)}, u32[]{:S(2)}, u32[]{:S(2)}) %collective-permute-start.5) | collective-permute-done | bytes 172064 | tf_op jit(solution)/shard_map/ppermute | solution.py:568
  29.6 0.0 copy-done
  29.6 0.0 copy-done.1
  29.6 11.4 %shard_map.99 = (f32[16,24,128]{2,1,0:T(8,128)}, f32[3,1,1,4096]{3,2,1,0:T(1,128)}) custom-call(s32[3]{0:T(128)S(1)} %pad_add_fusion.par_ref, f32[25,32,128]{2,1,0:T(8,128)S(1)} %get-tuple-element.20.e_ref, f32[17,16,128]{2,1,0:T(8,128)S(1)} %get-tuple-element.21.g_ref, f32[42,8,128]{2,1,0:T(8,128)S(1)} %collective-permute-done.4.r1_ref, ...), custom_call_target="tpu_custom_call" | custom-call | tf_op jit(solution)/shard_map/pallas_call | solution.py:549
Async XLA Ops:
  0.6 25.9 %copy-start.2 = (s32[1,1,4096]{2,1,0:T(1,128)S(1)}, s32[1,1,4096]{2,1,0:T(1,128)}, u32[]{:S(2)}) copy-start(s32[1,1,4096]{2,1,0:T(1,128)} %cell_ref.3) | copy-start | bytes 49156
  7.1 12.7 %collective-permute-start = (f32[5,48,128]{2,1,0:T(8,128)S(1)}, f32[5,48,128]{2,1,0:T(8,128)S(1)}, u32[]{:S(2)}, u32[]{:S(2)}) collective-permute-start(f32[5,48,128]{2,1,0:T(8,128)S(1)} %get-tuple-element.15), channel_id=1, source_target_pairs={{0,16},{16,0},{32,48},{48,32},{64,80},{80,64},{96,112},{112,96},{1... | collective-permute-start | bytes 368648 | tf_op jit(solution)/shard_map/ppermute | solution.py:568
  8.4 11.4 %collective-permute-start.1 = (f32[5,48,128]{2,1,0:T(8,128)S(1)}, f32[5,48,128]{2,1,0:T(8,128)S(1)}, u32[]{:S(2)}, u32[]{:S(2)}) collective-permute-start(f32[5,48,128]{2,1,0:T(8,128)S(1)} %get-tuple-element.16), channel_id=1, source_target_pairs={{0,240},{16,32},{32,16},{48,64},{64,48},{80,96},{96,80},{112,128},... | collective-permute-start | bytes 368648 | tf_op jit(solution)/shard_map/ppermute | solution.py:568
  10.0 6.9 %collective-permute-start.2 = (f32[16,128]{1,0:T(8,128)S(1)}, f32[16,128]{1,0:T(8,128)S(1)}, u32[]{:S(2)}, u32[]{:S(2)}) collective-permute-start(f32[16,128]{1,0:T(8,128)S(1)} %get-tuple-element.17), channel_id=1, source_target_pairs={{0,32},{16,48},{32,0},{48,16},{64,96},{80,112},{96,64},{112,80},{1... | collective-permute-start | bytes 24584 | tf_op jit(solution)/shard_map/ppermute | solution.py:568
  13.7 6.1 %collective-permute-start.3 = (f32[16,128]{1,0:T(8,128)S(1)}, f32[16,128]{1,0:T(8,128)S(1)}, u32[]{:S(2)}, u32[]{:S(2)}) collective-permute-start(f32[16,128]{1,0:T(8,128)S(1)} %get-tuple-element.18), channel_id=1, source_target_pairs={{0,224},{16,240},{32,64},{48,80},{64,32},{80,48},{96,128},{112,144... | collective-permute-start | bytes 24584 | tf_op jit(solution)/shard_map/ppermute | solution.py:568
  13.7 15.9 %copy-start = (bf16[4448,256]{1,0:T(8,128)(2,1)S(1)}, bf16[4448,256]{1,0:T(8,128)(2,1)}, u32[]{:S(2)}) copy-start(bf16[4448,256]{1,0:T(8,128)(2,1)} %constant.11.clone.packed_hbm.packed_ref) | copy-start | bytes 6832132
  13.7 15.9 %copy-start.1 = (f32[3,1,1,4096]{3,2,1,0:T(1,128)S(1)}, f32[3,1,1,4096]{3,2,1,0:T(1,128)}, u32[]{:S(2)}) copy-start(f32[3,1,1,4096]{3,2,1,0:T(1,128)} %frac_ref.1) | copy-start | bytes 147460
  20.5 6.6 %collective-permute-start.4 = (f32[42,8,128]{2,1,0:T(8,128)S(1)}, f32[42,8,128]{2,1,0:T(8,128)S(1)}, u32[]{:S(2)}, u32[]{:S(2)}) collective-permute-start(f32[42,8,128]{2,1,0:T(8,128)S(1)} %get-tuple-element.22), channel_id=1, source_target_pairs={{0,1},{1,0},{2,3},{3,2},{4,5},{5,4},{6,7},{7,6},{8,9},{9,8},{10,11... | collective-permute-start | bytes 516104 | tf_op jit(solution)/shard_map/ppermute | solution.py:568
  20.6 9.0 %collective-permute-start.5 = (f32[42,8,128]{2,1,0:T(8,128)S(1)}, f32[42,8,128]{2,1,0:T(8,128)S(1)}, u32[]{:S(2)}, u32[]{:S(2)}) collective-permute-start(f32[42,8,128]{2,1,0:T(8,128)S(1)} %get-tuple-element.23), channel_id=1, source_target_pairs={{0,15},{1,2},{2,1},{3,4},{4,3},{5,6},{6,5},{7,8},{8,7},{9,10},{10,... | collective-permute-start | bytes 516104 | tf_op jit(solution)/shard_map/ppermute | solution.py:568

commit v5 on v4

--- a/solution.py
+++ b/solution.py
@@ -542,7 +542,7 @@
             force_ref[k, 0, :, span] = -charge * sums[k]
         return carry
 
-    lax.fori_loop(0, ATOMS // TILE, step, 0)
+    lax.fori_loop(0, ATOMS // TILE, step, 0, unroll=True)
 
 
 def call(kernel, outs, args, spaces, scratch=(), dtype=F32):

time: 41.3 us -> 41.4 us (level)
  no operation moved by 1% of the time
where the time goes in v5:
time: 41.4 us; the launch traced here: 41.1 us
  Pallas kernels  21.6 us (52%)
  starting transfers between devices  12.7 us (31%)
  waiting for transfers between devices  5.39 us (13%)
  between operations  1.36 us (3%)
    pallas_call x5, Pallas kernels, call(): pl.pallas_call(kernel, out_shape=[jax.ShapeDtypeStruct(shape, dtype) for...  21.6 us
    ppermute x6, starting transfers between devices, swap(): return lax.ppermute(value, axis, pairs)  12.7 us
    ppermute x6, waiting for transfers between devices, swap(): return lax.ppermute(value, axis, pairs)  5.39 us
  transfers between devices with their start and end apart: 6, of which 2 were waited for; matrix products, arithmetic and copies ran while one was open for 0% of the time, Pallas kernels for 9%

profile of v5, /device:TPU:4, one launch (start us, length us, event | category | flops | bytes accessed | tf_op | source)
XLA Modules:
  0.0 41.1 jit_solution(17592923376830121429)
XLA Ops:
  0.6 0.0 copy-start.2
  1.3 0.1 pad_add_fusion.par_ref
  1.4 5.7 %shard_map.95 = (f32[17,32,128]{2,1,0:T(8,128)S(1)}, f32[9,16,128]{2,1,0:T(8,128)S(1)}, f32[5,48,128]{2,1,0:T(8,128)S(1)}, f32[5,48,128]{2,1,0:T(8,128)S(1)}, f3...) custom-call(s32[3]{0:T(128)S(1)} %pad_add_fusion.par_ref, s32[1,1]{1,0:T(1,128)S(6)} %copy.10.count_ref, ...), custom_call_target="tpu_custom_call" | custom-call | tf_op jit(solution)/shard_map/pallas_call | solution.py:549
  7.1 1.3 %collective-permute-start = (f32[5,48,128]{2,1,0:T(8,128)S(1)}, f32[5,48,128]{2,1,0:T(8,128)S(1)}, u32[]{:S(2)}, u32[]{:S(2)}) collective-permute-start(f32[5,48,128]{2,1,0:T(8,128)S(1)} %get-tuple-element.15), channel_id=1, source_target_pairs={{0,16},{16,0},{32,48},{48,32},{64,80},{80,64},{96,112},{112,96},{1... | collective-permute-start | bytes 368648 | tf_op jit(solution)/shard_map/ppermute | solution.py:568
  8.4 1.6 %collective-permute-start.1 = (f32[5,48,128]{2,1,0:T(8,128)S(1)}, f32[5,48,128]{2,1,0:T(8,128)S(1)}, u32[]{:S(2)}, u32[]{:S(2)}) collective-permute-start(f32[5,48,128]{2,1,0:T(8,128)S(1)} %get-tuple-element.16), channel_id=1, source_target_pairs={{0,240},{16,32},{32,16},{48,64},{64,48},{80,96},{96,80},{112,128},... | collective-permute-start | bytes 368648 | tf_op jit(solution)/shard_map/ppermute | solution.py:568
  10.0 3.7 %collective-permute-start.2 = (f32[16,128]{1,0:T(8,128)S(1)}, f32[16,128]{1,0:T(8,128)S(1)}, u32[]{:S(2)}, u32[]{:S(2)}) collective-permute-start(f32[16,128]{1,0:T(8,128)S(1)} %get-tuple-element.17), channel_id=1, source_target_pairs={{0,32},{16,48},{32,0},{48,16},{64,96},{80,112},{96,64},{112,80},{1... | collective-permute-start | bytes 24584 | tf_op jit(solution)/shard_map/ppermute | solution.py:568
  13.7 0.0 collective-permute-start.3
  13.7 0.0 copy-start
  13.7 0.0 copy-start.1
  13.7 3.2 %shard_map.96.h_ref = f32[9,40,256]{2,1,0:T(8,128)S(1)} custom-call(f32[9,9,9]{2,1,0:T(8,128)} %fine_hbm.1, f32[9,9,9]{2,1,0:T(8,128)} %middle_hbm.1, f32[9,9,9]{2,1,0:T(8,128)} %coarse_hbm.1, bf16[4448,256]{1,0:T(8,128)(2,1)} %constant.11.clone.packed_hbm.packed_ref, f32[1,1,4096]{2,1,0:T(1,128)S(1)} %get-tuple-element.19.live_ref.charge_ref), custom_call_target="tpu_custom_call" | custom-call | tf_op jit(solution)/shard_map/pallas_call | solution.py:549
  16.9 0.0 collective-permute-done.2.rt1_ref
  16.9 2.9 %collective-permute-done.3.rt2_ref = f32[16,128]{1,0:T(8,128)S(1)} collective-permute-done((f32[16,128]{1,0:T(8,128)S(1)}, f32[16,128]{1,0:T(8,128)S(1)}, u32[]{:S(2)}, u32[]{:S(2)}) %collective-permute-start.3) | collective-permute-done | bytes 8224 | tf_op jit(solution)/shard_map/ppermute | solution.py:568
  19.8 0.0 collective-permute-done.r1_ref
  19.8 0.0 collective-permute-done.1.r2_ref
  19.8 0.7 %shard_map.97 = (f32[25,32,128]{2,1,0:T(8,128)S(1)}, f32[17,16,128]{2,1,0:T(8,128)S(1)}, f32[42,8,128]{2,1,0:T(8,128)S(1)}, f32[42,8,128]{2,1,0:T(8,128)S(1)}) custom-call(s32[3]{0:T(128)S(1)} %pad_add_fusion.par_ref, f32[17,32,128]{2,1,0:T(8,128)S(1)} %get-tuple-element.13.shat_ref, f32[9,16,128]{2,1,0:T(8,128)S(1)} %get-tuple-element.14.mc_ref, ...), custom_call_target="tpu_custom_call" | custom-call | tf_op jit(solution)/shard_map/pallas_call | solution.py:549
  20.5 0.1 collective-permute-start.4
  20.6 6.0 %collective-permute-start.5 = (f32[42,8,128]{2,1,0:T(8,128)S(1)}, f32[42,8,128]{2,1,0:T(8,128)S(1)}, u32[]{:S(2)}, u32[]{:S(2)}) collective-permute-start(f32[42,8,128]{2,1,0:T(8,128)S(1)} %get-tuple-element.23), channel_id=1, source_target_pairs={{0,15},{1,2},{2,1},{3,4},{4,3},{5,6},{6,5},{7,8},{8,7},{9,10},{10,... | collective-permute-start | bytes 516104 | tf_op jit(solution)/shard_map/ppermute | solution.py:568
  26.5 0.0 copy-done.2
  26.5 0.6 %shard_map.98.hot_ref = bf16[384,4096]{1,0:T(8,128)(2,1)S(1)} custom-call(s32[1,1,4096]{2,1,0:T(1,128)S(1)} %copy-done.2, f32[25,32,128]{2,1,0:T(8,128)S(1)} %get-tuple-element.20.e_ref), custom_call_target="tpu_custom_call" | custom-call | tf_op jit(solution)/shard_map/pallas_call | solution.py:549
  27.1 0.0 collective-permute-done.4.r1_ref
  27.1 2.5 %collective-permute-done.5.r2_ref = f32[42,8,128]{2,1,0:T(8,128)S(1)} collective-permute-done((f32[42,8,128]{2,1,0:T(8,128)S(1)}, f32[42,8,128]{2,1,0:T(8,128)S(1)}, u32[]{:S(2)}, u32[]{:S(2)}) %collective-permute-start.5) | collective-permute-done | bytes 172064 | tf_op jit(solution)/shard_map/ppermute | solution.py:568
  29.6 0.0 copy-done
  29.6 0.0 copy-done.1
  29.6 11.5 %shard_map.99 = (f32[16,24,128]{2,1,0:T(8,128)}, f32[3,1,1,4096]{3,2,1,0:T(1,128)}) custom-call(s32[3]{0:T(128)S(1)} %pad_add_fusion.par_ref, f32[25,32,128]{2,1,0:T(8,128)S(1)} %get-tuple-element.20.e_ref, f32[17,16,128]{2,1,0:T(8,128)S(1)} %get-tuple-element.21.g_ref, f32[42,8,128]{2,1,0:T(8,128)S(1)} %collective-permute-done.4.r1_ref, ...), custom_call_target="tpu_custom_call" | custom-call | tf_op jit(solution)/shard_map/pallas_call | solution.py:549
Async XLA Ops:
  0.6 25.9 %copy-start.2 = (s32[1,1,4096]{2,1,0:T(1,128)S(1)}, s32[1,1,4096]{2,1,0:T(1,128)}, u32[]{:S(2)}) copy-start(s32[1,1,4096]{2,1,0:T(1,128)} %cell_ref.3) | copy-start | bytes 49156
  7.1 12.7 %collective-permute-start = (f32[5,48,128]{2,1,0:T(8,128)S(1)}, f32[5,48,128]{2,1,0:T(8,128)S(1)}, u32[]{:S(2)}, u32[]{:S(2)}) collective-permute-start(f32[5,48,128]{2,1,0:T(8,128)S(1)} %get-tuple-element.15), channel_id=1, source_target_pairs={{0,16},{16,0},{32,48},{48,32},{64,80},{80,64},{96,112},{112,96},{1... | collective-permute-start | bytes 368648 | tf_op jit(solution)/shard_map/ppermute | solution.py:568
  8.4 11.4 %collective-permute-start.1 = (f32[5,48,128]{2,1,0:T(8,128)S(1)}, f32[5,48,128]{2,1,0:T(8,128)S(1)}, u32[]{:S(2)}, u32[]{:S(2)}) collective-permute-start(f32[5,48,128]{2,1,0:T(8,128)S(1)} %get-tuple-element.16), channel_id=1, source_target_pairs={{0,240},{16,32},{32,16},{48,64},{64,48},{80,96},{96,80},{112,128},... | collective-permute-start | bytes 368648 | tf_op jit(solution)/shard_map/ppermute | solution.py:568
  10.0 6.9 %collective-permute-start.2 = (f32[16,128]{1,0:T(8,128)S(1)}, f32[16,128]{1,0:T(8,128)S(1)}, u32[]{:S(2)}, u32[]{:S(2)}) collective-permute-start(f32[16,128]{1,0:T(8,128)S(1)} %get-tuple-element.17), channel_id=1, source_target_pairs={{0,32},{16,48},{32,0},{48,16},{64,96},{80,112},{96,64},{112,80},{1... | collective-permute-start | bytes 24584 | tf_op jit(solution)/shard_map/ppermute | solution.py:568
  13.7 6.1 %collective-permute-start.3 = (f32[16,128]{1,0:T(8,128)S(1)}, f32[16,128]{1,0:T(8,128)S(1)}, u32[]{:S(2)}, u32[]{:S(2)}) collective-permute-start(f32[16,128]{1,0:T(8,128)S(1)} %get-tuple-element.18), channel_id=1, source_target_pairs={{0,224},{16,240},{32,64},{48,80},{64,32},{80,48},{96,128},{112,144... | collective-permute-start | bytes 24584 | tf_op jit(solution)/shard_map/ppermute | solution.py:568
  13.7 15.9 %copy-start = (bf16[4448,256]{1,0:T(8,128)(2,1)S(1)}, bf16[4448,256]{1,0:T(8,128)(2,1)}, u32[]{:S(2)}) copy-start(bf16[4448,256]{1,0:T(8,128)(2,1)} %constant.11.clone.packed_hbm.packed_ref) | copy-start | bytes 6832132
  13.7 15.9 %copy-start.1 = (f32[3,1,1,4096]{3,2,1,0:T(1,128)S(1)}, f32[3,1,1,4096]{3,2,1,0:T(1,128)}, u32[]{:S(2)}) copy-start(f32[3,1,1,4096]{3,2,1,0:T(1,128)} %frac_ref.1) | copy-start | bytes 147460
  20.5 6.6 %collective-permute-start.4 = (f32[42,8,128]{2,1,0:T(8,128)S(1)}, f32[42,8,128]{2,1,0:T(8,128)S(1)}, u32[]{:S(2)}, u32[]{:S(2)}) collective-permute-start(f32[42,8,128]{2,1,0:T(8,128)S(1)} %get-tuple-element.22), channel_id=1, source_target_pairs={{0,1},{1,0},{2,3},{3,2},{4,5},{5,4},{6,7},{7,6},{8,9},{9,8},{10,11... | collective-permute-start | bytes 516104 | tf_op jit(solution)/shard_map/ppermute | solution.py:568
  20.6 9.0 %collective-permute-start.5 = (f32[42,8,128]{2,1,0:T(8,128)S(1)}, f32[42,8,128]{2,1,0:T(8,128)S(1)}, u32[]{:S(2)}, u32[]{:S(2)}) collective-permute-start(f32[42,8,128]{2,1,0:T(8,128)S(1)} %get-tuple-element.23), channel_id=1, source_target_pairs={{0,15},{1,2},{2,1},{3,4},{4,3},{5,6},{6,5},{7,8},{8,7},{9,10},{10,... | collective-permute-start | bytes 516104 | tf_op jit(solution)/shard_map/ppermute | solution.py:568
